TPU v7x, 128 devices: a whole 4x4x4 slice. The times are simulated.
128 devices in a mesh: ctx: 16 (over x, y), fsdp: 8 (over z, core).
Axes of the slice: x: 4, y: 4, z: 4, core: 2. Of those that a mesh axis runs over, the one named last changes fastest.
Arguments:
- hidden: bfloat16 [16, 8, 128, 960], P('ctx', 'fsdp'), may hold values from -6 to 6
- cotangent: bfloat16 [16, 8, 128, 960], P('ctx', 'fsdp'), may hold values from -6 to 6
- pairing: int32 [16], replicated, may hold values from 0 to 15, as said below
- documents: int32 [16, 8, 128], P(None, 'fsdp'), may hold values from 0 to 3, as said below
- attn_gain: bfloat16 [960], P('fsdp'), may hold values from 0.5 to 1.5
- w_query: bfloat16 [960, 960], P('fsdp'), may hold values from -0.1875 to 0.1875
- w_key: bfloat16 [960, 320], P('fsdp'), may hold values from -0.1875 to 0.1875
- w_value: bfloat16 [960, 320], P('fsdp'), may hold values from -0.1875 to 0.1875
- w_out: bfloat16 [960, 960], P('fsdp'), may hold values from -3 to 3
- mlp_gain: bfloat16 [960], P('fsdp'), may hold values from 0.5 to 1.5
- w_gate: bfloat16 [960, 2560], P('fsdp'), may hold values from -0.1875 to 0.1875
- w_up: bfloat16 [960, 2560], P('fsdp'), may hold values from -0.1875 to 0.1875
- w_down: bfloat16 [2560, 960], P('fsdp'), may hold values from -0.125 to 0.125
Outputs:
- result: bfloat16 [16, 8, 128, 960], P('ctx', 'fsdp')
- input_grad: bfloat16 [16, 8, 128, 960], P('ctx', 'fsdp')
- grad_attn_gain: float32 [960], P('fsdp')
- grad_query: float32 [960, 960], P('fsdp')
- grad_key: float32 [960, 320], P('fsdp')
- grad_value: float32 [960, 320], P('fsdp')
- grad_out: float32 [960, 960], P('fsdp')
- grad_mlp_gain: float32 [960], P('fsdp')
- grad_gate: float32 [960, 2560], P('fsdp')
- grad_up: float32 [960, 2560], P('fsdp')
- grad_down: float32 [2560, 960], P('fsdp')
Inputs may be any that keep to these rules, and one draw needn't show every extreme that they name: A permutation: each value once; index c of ctx holds blocks pairing[c] and 31 - pairing[c] of every sequence. `documents`: taken in order of pos, a sequence's ids never fall; document 0 holds at least places 0 to 1023, and the last place is in document 3.
All inputs are finite; a program needn't handle non-finite values.
Results may differ from a plain program's by a relative error of at most 0.025.
Values may be sent and summed in bfloat16 or wider, within the bound.
No kernel may reach another device: no remote copies, remote signals or barrier semaphores. Data moves between devices by JAX's collectives and lax.ppermute only.
A program may use at most 128 MiB of HBM per device.

v0:
```python
import jax
import jax.numpy as jnp
from jax import lax
from jax.sharding import PartitionSpec as P

QUERY_HEADS = 15
KEY_VALUE_HEADS = 5
HEAD_SIZE = 64


EPSILON = 1e-05
NEGATIVE = -1e30
ROPE_BASE = 10000.0


def seq_positions(pairing, row_count):
    half_rows = row_count // 2
    count_pairs = pairing.shape[0]
    offsets = jnp.arange(row_count, dtype=jnp.int32)
    early_rows = pairing[:, None] * half_rows + offsets[None, :]
    late_rows = (2 * count_pairs - 1 - pairing[:, None]) * half_rows + offsets[None, :] - half_rows
    return jnp.where(offsets[None, :] < half_rows, early_rows, late_rows)


def rotary(head_dim, positions):
    frequency = ROPE_BASE ** (-(jnp.arange(head_dim // 2, dtype=jnp.float32) * 2.0) / head_dim)
    angles = positions.astype(jnp.float32)[:, None] * frequency[None, :]
    return (jnp.cos(angles), jnp.sin(angles))


def apply_rotary(value_rows, cosine_table, sine_lookup, head_count):
    row_count = value_rows.shape[0]
    heads_view = value_rows.reshape(row_count, head_count, -1)
    half_dim = heads_view.shape[-1] // 2
    first_half = heads_view[..., :half_dim]
    second = heads_view[..., half_dim:]
    cos_view = cosine_table[:, None, :]
    sin_view = sine_lookup[:, None, :]
    rotated = jnp.concatenate(
        [first_half * cos_view - second * sin_view, second * cos_view + first_half * sin_view],
        axis=-1,
    )
    return rotated.reshape(row_count, -1)


def plain_dot(left, right):
    return jnp.dot(left, right, preferred_element_type=jnp.float32)


def left_dot(left, right):
    return lax.dot_general(
        left, right, (((0,), (0,)), ((), ())), preferred_element_type=jnp.float32
    )


def right_dot(left, right):
    return lax.dot_general(
        left, right, (((1,), (1,)), ((), ())), preferred_element_type=jnp.float32
    )


def split_heads(value_rows, row_count, key_value_count, query_group_width, head_dim):
    return (
        value_rows.reshape(row_count, key_value_count, query_group_width, head_dim)
        .transpose(1, 2, 0, 3)
        .reshape(key_value_count, query_group_width * row_count, head_dim)
    )


def merge_heads(value_rows, row_count, key_value_count, query_group_width, head_dim):
    return (
        value_rows.reshape(key_value_count, query_group_width, row_count, head_dim)
        .transpose(2, 0, 1, 3)
        .reshape(row_count, key_value_count * query_group_width * head_dim)
    )


def norm_back(grad_normed, normed, inv_rms, gain):
    scaled = grad_normed * gain.astype(jnp.float32)
    return inv_rms * (scaled - normed * jnp.mean(scaled * normed, axis=1, keepdims=True))


def per_device(
    hidden,
    cotangent,
    pairing,
    documents,
    attn_gain,
    w_query,
    w_key,
    w_value,
    w_out,
    mlp_gain,
    w_gate,
    w_up,
    w_down,
):
    row_count = hidden.shape[2]
    model_width = hidden.shape[3]
    key_value_count = KEY_VALUE_HEADS
    query_group_width = QUERY_HEADS // KEY_VALUE_HEADS
    head_dim = HEAD_SIZE
    score_scale = head_dim ** (-0.5)
    ctx_index = lax.axis_index("ctx")
    positions = seq_positions(pairing, row_count)
    key_pos = positions.reshape(-1)
    key_doc = documents.reshape(-1)
    query_pos = lax.dynamic_index_in_dim(positions, ctx_index, 0, keepdims=False)
    query_doc = lax.dynamic_index_in_dim(documents[:, 0, :], ctx_index, 0, keepdims=False)
    allowed = (query_doc[:, None] == key_doc[None, :]) & (query_pos[:, None] >= key_pos[None, :])
    cosine_table, sine_lookup = rotary(head_dim, query_pos)
    inputs = hidden.reshape(row_count, model_width).astype(jnp.float32)
    gain_a, query_w, key_matrix, value_w, out_w = (
        lax.all_gather(attn_gain, "fsdp", axis=0, tiled=True),
        lax.all_gather(w_query, "fsdp", axis=0, tiled=True),
        lax.all_gather(w_key, "fsdp", axis=0, tiled=True),
        lax.all_gather(w_value, "fsdp", axis=0, tiled=True),
        lax.all_gather(w_out, "fsdp", axis=0, tiled=True),
    )
    inv_rms_a = lax.rsqrt(jnp.mean(inputs * inputs, axis=1, keepdims=True) + EPSILON)
    normed_a = inputs * inv_rms_a
    hidden_a = (normed_a * gain_a.astype(jnp.float32)).astype(jnp.bfloat16)
    query_rows = apply_rotary(
        plain_dot(hidden_a, query_w), cosine_table, sine_lookup, QUERY_HEADS
    ).astype(jnp.bfloat16)
    key_rows = apply_rotary(
        plain_dot(hidden_a, key_matrix), cosine_table, sine_lookup, key_value_count
    ).astype(jnp.bfloat16)
    value_rows = plain_dot(hidden_a, value_w).astype(jnp.bfloat16)
    all_keys, all_values = (
        lax.all_gather(key_rows, "ctx", axis=0, tiled=True),
        lax.all_gather(value_rows, "ctx", axis=0, tiled=True),
    )
    length = all_keys.shape[0]
    query_split = split_heads(query_rows, row_count, key_value_count, query_group_width, head_dim)
    key_split = all_keys.reshape(length, key_value_count, head_dim).transpose(1, 0, 2)
    value_split = all_values.reshape(length, key_value_count, head_dim).transpose(1, 0, 2)

    def head_scores(query_head, key_head):
        scores = right_dot(query_head, key_head) * score_scale
        scores = scores.reshape(query_group_width, row_count, length)
        return jnp.where(allowed[None], scores, NEGATIVE)

    def attend(pieces):
        query_head, key_head, value_head = pieces
        scores = head_scores(query_head, key_head)
        row_max = jnp.max(scores, axis=2, keepdims=True)
        row_total = jnp.sum(jnp.exp(scores - row_max), axis=2, keepdims=True)
        log_total = row_max + jnp.log(row_total)
        attn_probs = jnp.exp(scores - log_total).astype(jnp.bfloat16)
        attended = plain_dot(attn_probs.reshape(-1, length), value_head)
        return (attended, log_total[..., 0])

    head_outs, log_totals = lax.map(attend, (query_split, key_split, value_split))
    attn_rows = merge_heads(
        head_outs, row_count, key_value_count, query_group_width, head_dim
    ).astype(jnp.bfloat16)
    middle = inputs + plain_dot(attn_rows, out_w)
    gain_m, gate_w, up_w, down_w = (
        lax.all_gather(mlp_gain, "fsdp", axis=0, tiled=True),
        lax.all_gather(w_gate, "fsdp", axis=0, tiled=True),
        lax.all_gather(w_up, "fsdp", axis=0, tiled=True),
        lax.all_gather(w_down, "fsdp", axis=0, tiled=True),
    )
    inv_rms_m = lax.rsqrt(jnp.mean(middle * middle, axis=1, keepdims=True) + EPSILON)
    normed_m = middle * inv_rms_m
    hidden_m = (normed_m * gain_m.astype(jnp.float32)).astype(jnp.bfloat16)
    gate_pre = plain_dot(hidden_m, gate_w)
    up_pre = plain_dot(hidden_m, up_w)
    sigmoid_gate = jax.nn.sigmoid(gate_pre)
    activated = (gate_pre * sigmoid_gate * up_pre).astype(jnp.bfloat16)
    result = middle + plain_dot(activated, down_w)
    gain_m, gate_w, up_w, down_w = (
        lax.all_gather(mlp_gain, "fsdp", axis=0, tiled=True),
        lax.all_gather(w_gate, "fsdp", axis=0, tiled=True),
        lax.all_gather(w_up, "fsdp", axis=0, tiled=True),
        lax.all_gather(w_down, "fsdp", axis=0, tiled=True),
    )
    grad_rows = cotangent.reshape(row_count, model_width)
    grad_act = right_dot(grad_rows, down_w)
    grad_gate_pre = (
        grad_act * up_pre * sigmoid_gate * (1.0 + gate_pre * (1.0 - sigmoid_gate))
    ).astype(jnp.bfloat16)
    grad_up_pre = (grad_act * gate_pre * sigmoid_gate).astype(jnp.bfloat16)
    grad_hidden_m = right_dot(grad_gate_pre, gate_w) + right_dot(grad_up_pre, up_w)
    grad_gain_m = jnp.sum(grad_hidden_m * normed_m, axis=0)
    grad_middle = grad_rows.astype(jnp.float32) + norm_back(
        grad_hidden_m, normed_m, inv_rms_m, gain_m
    )
    grad_down = left_dot(activated, grad_rows)
    grad_gate = left_dot(hidden_m, grad_gate_pre)
    grad_up = left_dot(hidden_m, grad_up_pre)
    mlp_sums = (
        lax.psum_scatter(
            grad_gain_m.astype(jnp.bfloat16), "fsdp", scatter_dimension=0, tiled=True
        ).astype(jnp.float32),
        lax.psum_scatter(
            grad_gate.astype(jnp.bfloat16), "fsdp", scatter_dimension=0, tiled=True
        ).astype(jnp.float32),
        lax.psum_scatter(
            grad_up.astype(jnp.bfloat16), "fsdp", scatter_dimension=0, tiled=True
        ).astype(jnp.float32),
        lax.psum_scatter(
            grad_down.astype(jnp.bfloat16), "fsdp", scatter_dimension=0, tiled=True
        ).astype(jnp.float32),
    )
    gain_a, query_w, key_matrix, value_w, out_w = (
        lax.all_gather(attn_gain, "fsdp", axis=0, tiled=True),
        lax.all_gather(w_query, "fsdp", axis=0, tiled=True),
        lax.all_gather(w_key, "fsdp", axis=0, tiled=True),
        lax.all_gather(w_value, "fsdp", axis=0, tiled=True),
        lax.all_gather(w_out, "fsdp", axis=0, tiled=True),
    )
    grad_branch = grad_middle.astype(jnp.bfloat16)
    grad_attended = right_dot(grad_branch, out_w).astype(jnp.bfloat16)
    grad_split = split_heads(grad_attended, row_count, key_value_count, query_group_width, head_dim)

    def attend_back(pieces):
        query_head, key_head, value_head, grad_head, log_head = pieces
        scores = head_scores(query_head, key_head)
        attn_probs = jnp.exp(scores - log_head[..., None])
        grad_probs = right_dot(grad_head, value_head).reshape(query_group_width, row_count, length)
        row_inner = jnp.sum(attn_probs * grad_probs, axis=2, keepdims=True)
        grad_scores = (
            (attn_probs * (grad_probs - row_inner)).astype(jnp.bfloat16).reshape(-1, length)
        )
        low_probs = attn_probs.astype(jnp.bfloat16).reshape(-1, length)
        grad_query_head = plain_dot(grad_scores, key_head) * score_scale
        grad_key_head = left_dot(grad_scores, query_head) * score_scale
        grad_value_head = left_dot(low_probs, grad_head)
        return (grad_query_head, grad_key_head, grad_value_head)

    grad_q_heads, grad_k_heads, grad_v_heads = lax.map(
        attend_back, (query_split, key_split, value_split, grad_split, log_totals)
    )
    grad_q_rows = merge_heads(grad_q_heads, row_count, key_value_count, query_group_width, head_dim)
    grad_k_all = grad_k_heads.transpose(1, 0, 2).reshape(length, key_value_count * head_dim)
    grad_v_all = grad_v_heads.transpose(1, 0, 2).reshape(length, key_value_count * head_dim)
    key_sum, value_sum = (
        lax.psum_scatter(
            grad_k_all.astype(jnp.bfloat16), "ctx", scatter_dimension=0, tiled=True
        ).astype(jnp.float32),
        lax.psum_scatter(
            grad_v_all.astype(jnp.bfloat16), "ctx", scatter_dimension=0, tiled=True
        ).astype(jnp.float32),
    )
    grad_queries = apply_rotary(grad_q_rows, cosine_table, -sine_lookup, QUERY_HEADS).astype(
        jnp.bfloat16
    )
    grad_keys = apply_rotary(key_sum, cosine_table, -sine_lookup, key_value_count).astype(
        jnp.bfloat16
    )
    grad_values = value_sum.astype(jnp.bfloat16)
    grad_hidden_a = (
        right_dot(grad_queries, query_w)
        + right_dot(grad_keys, key_matrix)
        + right_dot(grad_values, value_w)
    )
    grad_gain_a = jnp.sum(grad_hidden_a * normed_a, axis=0)
    grad_input = grad_middle + norm_back(grad_hidden_a, normed_a, inv_rms_a, gain_a)
    grad_outw = left_dot(attn_rows, grad_branch)
    grad_query = left_dot(hidden_a, grad_queries)
    grad_key = left_dot(hidden_a, grad_keys)
    grad_value = left_dot(hidden_a, grad_values)
    attn_sums = (
        lax.psum_scatter(
            grad_gain_a.astype(jnp.bfloat16), "fsdp", scatter_dimension=0, tiled=True
        ).astype(jnp.float32),
        lax.psum_scatter(
            grad_query.astype(jnp.bfloat16), "fsdp", scatter_dimension=0, tiled=True
        ).astype(jnp.float32),
        lax.psum_scatter(
            grad_key.astype(jnp.bfloat16), "fsdp", scatter_dimension=0, tiled=True
        ).astype(jnp.float32),
        lax.psum_scatter(
            grad_value.astype(jnp.bfloat16), "fsdp", scatter_dimension=0, tiled=True
        ).astype(jnp.float32),
        lax.psum_scatter(
            grad_outw.astype(jnp.bfloat16), "fsdp", scatter_dimension=0, tiled=True
        ).astype(jnp.float32),
    )
    gain_a_sum = attn_sums[0]
    gain_m_sum = mlp_sums[0]
    totals = (
        lax.psum(gain_a_sum.astype(jnp.bfloat16), "ctx").astype(jnp.float32),
        lax.psum(attn_sums[1].astype(jnp.bfloat16), "ctx").astype(jnp.float32),
        lax.psum(attn_sums[2].astype(jnp.bfloat16), "ctx").astype(jnp.float32),
        lax.psum(attn_sums[3].astype(jnp.bfloat16), "ctx").astype(jnp.float32),
        lax.psum(attn_sums[4].astype(jnp.bfloat16), "ctx").astype(jnp.float32),
        lax.psum(gain_m_sum.astype(jnp.bfloat16), "ctx").astype(jnp.float32),
        lax.psum(mlp_sums[1].astype(jnp.bfloat16), "ctx").astype(jnp.float32),
        lax.psum(mlp_sums[2].astype(jnp.bfloat16), "ctx").astype(jnp.float32),
        lax.psum(mlp_sums[3].astype(jnp.bfloat16), "ctx").astype(jnp.float32),
    )
    result_out = result.astype(jnp.bfloat16).reshape(1, 1, row_count, model_width)
    input_out = grad_input.astype(jnp.bfloat16).reshape(1, 1, row_count, model_width)
    return (
        result_out,
        input_out,
        totals[0],
        totals[1],
        totals[2],
        totals[3],
        totals[4],
        totals[5],
        totals[6],
        totals[7],
        totals[8],
    )


def solution(mesh):
    placed = (
        P("ctx", "fsdp", None, None),
        P("ctx", "fsdp", None, None),
        P(),
        P(None, "fsdp", None),
        P("fsdp"),
        P("fsdp", None),
        P("fsdp", None),
        P("fsdp", None),
        P("fsdp", None),
        P("fsdp"),
        P("fsdp", None),
        P("fsdp", None),
        P("fsdp", None),
    )
    return jax.shard_map(
        per_device,
        mesh=mesh,
        in_specs=placed,
        out_specs=(
            P("ctx", "fsdp", None, None),
            P("ctx", "fsdp", None, None),
            P("fsdp"),
            P("fsdp", None),
            P("fsdp", None),
            P("fsdp", None),
            P("fsdp", None),
            P("fsdp"),
            P("fsdp", None),
            P("fsdp", None),
            P("fsdp", None),
        ),
        check_vma=False,
    )
```

profile of v0, /device:TPU:32, one launch (start us, length us, event | category | flops | bytes accessed | tf_op | source)
XLA Modules:
  0.0 914.2 jit_solution(17668322075877101008)
XLA Ops:
  11.0 12.5 %all-reduce.9 = (bf16[960]{0:T(1024)(128)(2,1)S(1)}, bf16[960]{0:T(1024)(128)(2,1)S(1)}) all-reduce(bf16[960]{0:T(1024)(128)(2,1)S(1)} %dynamic-update-slice, bf16[960]{0:T(1024)(128)(2,1)S(1)} %dynamic-update-slice.1), channel_id=1, replica_groups=mesh['ctx'=16,'fsdp'=8] {'fsdp'}, use_global_device_ids=true, to_apply=%add | all-reduce | flops 1920 | bytes 7680
  24.6 14.2 %all-gather = bf16[8,120,320]{1,2,0:T(8,128)(2,1)S(1)} all-gather(bf16[1,120,320]{1,2,0:T(8,128)(2,1)} %bitcast.318), channel_id=1, replica_groups=mesh['ctx'=16,'fsdp'=8] {'fsdp'}, dimensions={0}, use_global_device_ids=true | all-gather | bytes 691200 | tf_op jit(solution)/shard_map/all_gather | solution.py:116
  42.0 13.2 %all-gather.1 = bf16[8,120,320]{1,2,0:T(8,128)(2,1)S(1)} all-gather(bf16[1,120,320]{1,2,0:T(8,128)(2,1)S(1)} %bitcast.319), channel_id=1, replica_groups=mesh['ctx'=16,'fsdp'=8] {'fsdp'}, dimensions={0}, use_global_device_ids=true | all-gather | bytes 691200 | tf_op jit(solution)/shard_map/all_gather | solution.py:117
  60.2 27.5 %all-gather.12.cloned.1.call-done = bf16[2048,320]{0,1:T(8,128)(2,1)} async-done(((bf16[128,320]{0,1:T(8,128)(2,1)}), bf16[2048,320]{0,1:T(8,128)(2,1)}) %all-gather.12.cloned.1.call-update) | async-done | bytes 1310736 | tf_op jit(solution)/shard_map/all_gather | solution.py:131
  91.5 21.0 %all-gather.10.cloned.1.call-done = bf16[960,960]{1,0:T(8,128)(2,1)} async-done(((bf16[120,960]{1,0:T(8,128)(2,1)}), bf16[960,960]{1,0:T(8,128)(2,1)}) %all-gather.10.cloned.1.call-update) | async-done | bytes 1843216 | tf_op jit(solution)/shard_map/all_gather | solution.py:115
  116.5 44.5 %all-gather.14.cloned.1.call-done = bf16[2048,320]{0,1:T(8,128)(2,1)} async-done(((bf16[128,320]{0,1:T(8,128)(2,1)}), bf16[2048,320]{0,1:T(8,128)(2,1)}) %all-gather.14.cloned.1.call-update) | async-done | bytes 1310736 | tf_op jit(solution)/shard_map/all_gather | solution.py:132
  161.0 21.9 %while.30 = (s32[]{:T(128)}, bf16[5,384,64]{1,2,0:T(8,128)(2,1)S(1)}, f32[5,3,128]{2,1,0:T(4,128)S(1)}, bf16[5,384,64]{2,1,0:T(8,128)(2,1)S(1)}, bf16[5,2048,64]...) while((s32[]{:T(128)}, ...), condition=%wide.region_4.5_spmd.clone.clone, body=%wide.region_1.4_spmd.clone.sunk.clone | while | flops 207617664 | bytes 10978921 | solution.py:154
  188.3 34.7 %all-gather.18.cloned.1.call-done = bf16[960,2560]{1,0:T(8,128)(2,1)} async-done(((bf16[120,2560]{1,0:T(8,128)(2,1)}), bf16[960,2560]{1,0:T(8,128)(2,1)}) %all-gather.18.cloned.1.call-update) | async-done | bytes 4915216 | tf_op jit(solution)/shard_map/all_gather | solution.py:161
  223.0 4.3 fusion.106
  227.3 32.4 %all-gather.20.cloned.1.call-done = bf16[960,2560]{1,0:T(8,128)(2,1)} async-done(((bf16[120,2560]{1,0:T(8,128)(2,1)}), bf16[960,2560]{1,0:T(8,128)(2,1)}) %all-gather.20.cloned.1.call-update) | async-done | bytes 4915216 | tf_op jit(solution)/shard_map/all_gather | solution.py:162
  259.8 4.3 fusion.107
  264.1 34.0 %all-gather.22.cloned.1.call-done = bf16[2560,960]{1,0:T(8,128)(2,1)} async-done(((bf16[320,960]{1,0:T(8,128)(2,1)}), bf16[2560,960]{1,0:T(8,128)(2,1)}) %all-gather.22.cloned.1.call-update) | async-done | bytes 4915216 | tf_op jit(solution)/shard_map/all_gather | solution.py:163
  298.1 6.2 multiply_convert_fusion.1
  304.3 4.3 fusion.108
  312.2 77.1 %while.31 = (s32[]{:T(128)}, f32[5,384,64]{1,2,0:T(8,128)}, bf16[5,2048,64]{1,2,0:T(8,128)(2,1)}, bf16[5,2048,64]{1,2,0:T(8,128)(2,1)}, bf16[5,384,64]{2,1,0:T(8...) while((s32[]{:T(128)}, f32[5,384,64]{1,2,0:T(8,128)}, ...), condition=%wide.region_9.10_spmd.clone.clone, body=%wide.region_7.9_spmd.clone.sunk.clone | while | flops 614361472 | bytes 25608948 | solution.py:233
  316.6 4.9 multiply_convert_fusion.7
  331.9 5.1 multiply_convert_fusion.7
  347.4 4.9 multiply_convert_fusion.7
  362.7 5.0 multiply_convert_fusion.7
  378.1 4.9 multiply_convert_fusion.7
  395.0 71.6 %reduce-scatter.24.cloned.1.call-done = bf16[128,320]{1,0:T(8,128)(2,1)} async-done(((bf16[2048,320]{1,0:T(8,128)(2,1)}), bf16[128,320]{1,0:T(8,128)(2,1)}) %reduce-scatter.24.cloned.1.call-update) | async-done | bytes 81936
  469.0 73.7 %reduce-scatter.26.cloned.1.call-done = bf16[128,320]{1,0:T(8,128)(2,1)} async-done(((bf16[2048,320]{1,0:T(8,128)(2,1)}), bf16[128,320]{1,0:T(8,128)(2,1)}) %reduce-scatter.26.cloned.1.call-update) | async-done | bytes 81936
  563.9 42.4 %all-reduce.16.cloned.1.call-done = (bf16[960,320]{0,1:T(8,128)(2,1)}, bf16[960,320]{0,1:T(8,128)(2,1)}) async-done(((bf16[960,320]{0,1:T(8,128)(2,1)}, bf16[960,320]{0,1:T(8,128)(2,1)}), (bf16[960,320]{0,1:T(8,128)(2,1)}, bf16[960,320]{0,1:T(8,128)(2,1)})) %all-reduce.16.cloned.1.call-update) | async-done | bytes 1228816
  608.1 32.6 %reduce-scatter.14.cloned.1.call-done = bf16[120,960]{1,0:T(8,128)(2,1)} async-done(((bf16[960,960]{1,0:T(8,128)(2,1)}), bf16[120,960]{1,0:T(8,128)(2,1)}) %reduce-scatter.14.cloned.1.call-update) | async-done | bytes 230416 | tf_op jit(solution)/shard_map/reduce_scatter | solution.py:269
  640.7 34.8 %reduce-scatter.16.cloned.1.call-done = bf16[120,960]{1,0:T(8,128)(2,1)} async-done(((bf16[960,960]{1,0:T(8,128)(2,1)}), bf16[120,960]{1,0:T(8,128)(2,1)}) %reduce-scatter.16.cloned.1.call-update) | async-done | bytes 230416 | tf_op jit(solution)/shard_map/reduce_scatter | solution.py:278
  675.4 40.2 %reduce-scatter.18.cloned.1.call-done = bf16[120,2560]{1,0:T(8,128)(2,1)} async-done(((bf16[960,2560]{1,0:T(8,128)(2,1)}), bf16[120,2560]{1,0:T(8,128)(2,1)}) %reduce-scatter.18.cloned.1.call-update) | async-done | bytes 614416 | tf_op jit(solution)/shard_map/reduce_scatter | solution.py:197
  715.6 40.9 %reduce-scatter.20.cloned.1.call-done = bf16[120,2560]{1,0:T(8,128)(2,1)} async-done(((bf16[960,2560]{1,0:T(8,128)(2,1)}), bf16[120,2560]{1,0:T(8,128)(2,1)}) %reduce-scatter.20.cloned.1.call-update) | async-done | bytes 614416 | tf_op jit(solution)/shard_map/reduce_scatter | solution.py:200
  756.5 41.6 %reduce-scatter.22.cloned.1.call-done = bf16[320,960]{1,0:T(8,128)(2,1)} async-done(((bf16[2560,960]{1,0:T(8,128)(2,1)}), bf16[320,960]{1,0:T(8,128)(2,1)}) %reduce-scatter.22.cloned.1.call-update) | async-done | bytes 614416 | tf_op jit(solution)/shard_map/reduce_scatter | solution.py:203
  798.2 5.0 fusion.66
  805.5 14.4 %all-reduce.8 = (bf16[960]{0:T(1024)(128)(2,1)S(1)}, bf16[960]{0:T(1024)(128)(2,1)S(1)}) all-reduce(bf16[960]{0:T(1024)(128)(2,1)S(1)} %get-tuple-element.247, bf16[960]{0:T(1024)(128)(2,1)S(1)} %copy-done.38), channel_id=4, replica_groups=mesh['ctx'=16,'fsdp'=8] {'fsdp'}, use_global_device_ids=true, to_apply=%region_14.15.clone | all-reduce | flops 1920 | bytes 7680
  820.0 40.4 %all-reduce.6 = (bf16[120]{0:T(256)(128)(2,1)S(1)}, bf16[120]{0:T(256)(128)(2,1)S(1)}) all-reduce(bf16[120]{0:T(256)(128)(2,1)S(1)} %dynamic-slice.4, bf16[120]{0:T(256)(128)(2,1)S(1)} %dynamic-slice.10), channel_id=1, replica_groups=mesh['ctx'=16,'fsdp'=8] {'ctx'}, use_global_device_ids=true, to_apply=%region_15.16 | all-reduce | flops 240 | bytes 960 | tf_op jit(solution)/shard_map/psum | solution.py:285
  862.4 37.6 %all-reduce.14.cloned.1.call-done = (bf16[120,960]{1,0:T(8,128)(2,1)}, bf16[120,320]{0,1:T(8,128)(2,1)}, bf16[120,320]{0,1:T(8,128)(2,1)}, bf16[120,960]{1,0:T(8...) async-done(((bf16[120,960]{1,0:T(8,128)(2,1)}, bf16[120,320]{0,1:T(8,128)(2,1)}, bf16[120,320]{0,1:T(8,128)(2,1)}, ...) | async-done | bytes 2457616 | tf_op jit(solution)/shard_map/psum | solution.py:286
  (290 shorter events, 144.5 us)
Async XLA Ops:
  7.2 32.8 %copy-start = (bf16[1,1,128,960]{2,3,1,0:T(8,128)(2,1)S(1)}, bf16[1,1,128,960]{2,3,1,0:T(8,128)(2,1)}, u32[]{:S(2)}) copy-start(bf16[1,1,128,960]{2,3,1,0:T(8,128)(2,1)} %param.17) | copy-start | bytes 737284
  7.2 32.6 %copy-start.39 = (s32[16]{0:T(128)S(1)}, s32[16]{0:T(128)}, u32[]{:S(2)}) copy-start(s32[16]{0:T(128)} %param.19) | copy-start | bytes 196
  7.2 80.5 %all-gather.12.cloned.1.call-start = ((), (), s32[]{:S(2)}) async-start(), calls=%async_computation.8 | async-start | bytes 1392640 | tf_op jit(solution)/shard_map/all_gather | solution.py:131
  39.8 15.9 %copy-start.13 = (bf16[960,320]{0,1:T(8,128)(2,1)}, bf16[960,320]{0,1:T(8,128)(2,1)S(1)}, u32[]{:S(2)}) copy-start(bf16[960,320]{0,1:T(8,128)(2,1)S(1)} %reshape.400) | copy-start | bytes 1843204
  41.2 71.3 %all-gather.10.cloned.1.call-start = ((), (), s32[]{:S(2)}) async-start(), calls=%async_computation.7 | async-start | bytes 2211840 | tf_op jit(solution)/shard_map/all_gather | solution.py:115
  41.9 119.0 %all-gather.14.cloned.1.call-start = ((), (), s32[]{:S(2)}) async-start(), calls=%async_computation.9 | async-start | bytes 1392640 | tf_op jit(solution)/shard_map/all_gather | solution.py:132
  56.2 35.3 %copy-start.20 = (bf16[960,320]{0,1:T(8,128)(2,1)}, bf16[960,320]{0,1:T(8,128)(2,1)S(1)}, u32[]{:S(2)}) copy-start(bf16[960,320]{0,1:T(8,128)(2,1)S(1)} %reshape.402) | copy-start | bytes 1843204
  57.3 128.3 %all-gather.16.cloned.1.call-start = ((), (), s32[]{:S(2)}) async-start(), calls=%async_computation.10 | async-start | bytes 2211840 | tf_op jit(solution)/shard_map/all_gather | solution.py:118
  57.9 165.1 %all-gather.18.cloned.1.call-start = ((), (), s32[]{:S(2)}) async-start(), calls=%async_computation.11 | async-start | bytes 5529600 | tf_op jit(solution)/shard_map/all_gather | solution.py:161
  58.5 201.3 %all-gather.20.cloned.1.call-start = ((), (), s32[]{:S(2)}) async-start(), calls=%async_computation.12 | async-start | bytes 5529600 | tf_op jit(solution)/shard_map/all_gather | solution.py:162
  59.1 239.0 %all-gather.22.cloned.1.call-start = ((), (), s32[]{:S(2)}) async-start(), calls=%async_computation.13 | async-start | bytes 5898240 | tf_op jit(solution)/shard_map/all_gather | solution.py:163
  59.8 406.8 %reduce-scatter.24.cloned.1.call-start = ((), (), s32[]{:S(2)}) async-start(), calls=%async_computation.19 | async-start | bytes 1671168
  183.0 44.3 %copy-start.22 = (bf16[128,5,3,64]{0,3,2,1:T(8,128)(2,1)}, bf16[128,5,3,64]{0,3,2,1:T(8,128)(2,1)S(1)}, u32[]{:S(2)}) copy-start(bf16[128,5,3,64]{0,3,2,1:T(8,128)(2,1)S(1)} %copy.58) | copy-start | bytes 737284
  188.1 122.7 %copy-start.3 = (f32[128,960]{0,1:T(8,128)}, f32[128,960]{0,1:T(8,128)S(1)}, u32[]{:S(2)}) copy-start(f32[128,960]{0,1:T(8,128)S(1)} %get-tuple-element.341) | copy-start | bytes 1474564
  188.3 71.5 %copy-start.5 = (bf16[128,960]{0,1:T(8,128)(2,1)}, bf16[128,960]{0,1:T(8,128)(2,1)S(1)}, u32[]{:S(2)}) copy-start(bf16[128,960]{0,1:T(8,128)(2,1)S(1)} %multiply_convert_fusion.4) | copy-start | bytes 737284
  227.3 70.8 %copy-start.26 = (bf16[1,1,128,960]{2,3,1,0:T(8,128)(2,1)S(1)}, bf16[1,1,128,960]{2,3,1,0:T(8,128)(2,1)}, u32[]{:S(2)}) copy-start(bf16[1,1,128,960]{2,3,1,0:T(8,128)(2,1)} %param.18) | copy-start | bytes 737284
  304.3 4.4 copy-start.16
  304.3 4.4 copy-start.18
  304.3 4.4 copy-start.2
  391.9 150.8 %reduce-scatter.26.cloned.1.call-start = ((), (), s32[]{:S(2)}) async-start(), calls=%async_computation.20 | async-start | bytes 1671168
  394.7 73.0 %copy-start.1 = (bf16[1,1,128,960]{2,3,1,0:T(8,128)(2,1)S(1)}, bf16[1,1,128,960]{2,3,1,0:T(8,128)(2,1)}, u32[]{:S(2)}) copy-start(bf16[1,1,128,960]{2,3,1,0:T(8,128)(2,1)} %param.17) | copy-start | bytes 737284
  394.7 211.6 %all-reduce.16.cloned.1.call-start = ((), (), s32[]{:S(2)}) async-start(), calls=%async_computation.22 | async-start | bytes 2621440
  545.0 95.6 %reduce-scatter.14.cloned.1.call-start = ((), (), s32[]{:S(2)}) async-start(), calls=%async_computation.14 | async-start | bytes 2211840 | tf_op jit(solution)/shard_map/reduce_scatter | solution.py:269
  547.3 128.2 %reduce-scatter.16.cloned.1.call-start = ((), (), s32[]{:S(2)}) async-start(), calls=%async_computation.15 | async-start | bytes 2211840 | tf_op jit(solution)/shard_map/reduce_scatter | solution.py:278
  549.4 166.2 %reduce-scatter.18.cloned.1.call-start = ((), (), s32[]{:S(2)}) async-start(), calls=%async_computation.16 | async-start | bytes 5529600 | tf_op jit(solution)/shard_map/reduce_scatter | solution.py:197
  553.1 203.3 %reduce-scatter.20.cloned.1.call-start = ((), (), s32[]{:S(2)}) async-start(), calls=%async_computation.17 | async-start | bytes 5529600 | tf_op jit(solution)/shard_map/reduce_scatter | solution.py:200
  557.8 240.3 %reduce-scatter.22.cloned.1.call-start = ((), (), s32[]{:S(2)}) async-start(), calls=%async_computation.18 | async-start | bytes 5898240 | tf_op jit(solution)/shard_map/reduce_scatter | solution.py:203
  562.9 235.2 %copy-start.4 = (f32[128,960]{0,1:T(8,128)S(1)}, f32[128,960]{0,1:T(8,128)}, u32[]{:S(2)}) copy-start(f32[128,960]{0,1:T(8,128)} %copy-done.3) | copy-start | bytes 1474564
  562.9 337.0 %all-reduce.14.cloned.1.call-start = ((), (), s32[]{:S(2)}) async-start(), calls=%async_computation.21 | async-start | bytes 5079040 | tf_op jit(solution)/shard_map/psum | solution.py:286
  798.2 5.0 copy-start.14
  798.2 5.4 copy-start.21
  798.2 5.4 copy-start.32
  (40 other events, 105.4 us)
Sparse Core Ops, SparseCore 0:
  41.3 46.3 all-gather.11
  89.3 23.0 all-gather.9
  115.2 45.7 all-gather.13
  162.5 23.0 all-gather.15
  187.2 35.7 all-gather.17
  224.5 35.1 all-gather.19
  261.5 36.5 all-gather.21
  392.1 74.4 reduce-scatter.23
  469.8 72.8 reduce-scatter.25
  545.5 60.6 all-reduce.15
  608.7 31.8 reduce-scatter.13
  643.1 32.3 reduce-scatter.15
  677.9 37.6 reduce-scatter.17
  717.9 38.5 reduce-scatter.19
  758.7 39.3 reduce-scatter.21
  802.9 97.0 all-reduce.13
where the time goes:
time: 917 us; the launch traced here: 914 us
  waiting for transfers between devices  615 us (67%)
  matrix products  145 us (16%)
  blocking collectives  94.7 us (10%)
  local copies, waits for them, and re-layouts  24 us (3%)
  other arithmetic  18.1 us (2%)
  between operations  15.9 us (2%)
    unnamed x19, waiting for transfers between devices  191 us
    all_gather x1, waiting for transfers between devices, per_device(): lax.all_gather(value_rows, 'ctx', axis=0, tiled=True)  44.5 us
    dot_general x17, matrix products, right_dot(): lax.dot_general(left, right, (((1,), (1,)), ((), ())), preferred_element_...  42.7 us
    reduce_scatter x1, waiting for transfers between devices, per_device(): lax.psum_scatter(grad_down.astype(jnp.bfloat16), 'fsdp', scatter_dimensio...  41.6 us
    reduce_scatter x1, waiting for transfers between devices, per_device(): lax.psum_scatter(grad_up.astype(jnp.bfloat16), 'fsdp', scatter_dimension=...  40.9 us
    psum x1, blocking collectives, per_device(): lax.psum(gain_a_sum.astype(jnp.bfloat16), 'ctx').astype(jnp.float32)  40.4 us
    reduce_scatter x1, waiting for transfers between devices, per_device(): lax.psum_scatter(grad_gate.astype(jnp.bfloat16), 'fsdp', scatter_dimensio...  40.2 us
    dot_general x17, matrix products, left_dot(): lax.dot_general(left, right, (((0,), (0,)), ((), ())), preferred_element_...  38.9 us
  transfers between devices with their start and end apart: 16, of which 16 were waited for; matrix products, arithmetic and copies ran while one was open for 8% of the time, Pallas kernels for 0%

commit v1 on v0

v1 whole, which is shorter than its diff:
```python
import jax
import jax.numpy as jnp
from jax import lax
from jax.experimental import pallas as pl
from jax.experimental.pallas import tpu as pltpu
from jax.sharding import PartitionSpec as P

QUERY_HEADS = 15
KEY_VALUE_HEADS = 5
HEAD_SIZE = 64
GROUP = QUERY_HEADS // KEY_VALUE_HEADS

EPSILON = 1e-05
NEGATIVE = -1e30
ROPE_BASE = 10000.0

CTX = ("x", "y")
FSDP = ("z", "core")
KD = KEY_VALUE_HEADS * HEAD_SIZE
QD = QUERY_HEADS * HEAD_SIZE
PADDED = 1664

bf16, f32 = jnp.bfloat16, jnp.float32


def seq_positions(pairing, row_count):
    half_rows = row_count // 2
    count_pairs = pairing.shape[0]
    offsets = jnp.arange(row_count, dtype=jnp.int32)
    early_rows = pairing[:, None] * half_rows + offsets[None, :]
    late_rows = (2 * count_pairs - 1 - pairing[:, None]) * half_rows + offsets[None, :] - half_rows
    return jnp.where(offsets[None, :] < half_rows, early_rows, late_rows)


def rope_tables(positions):
    frequency = ROPE_BASE ** (-(jnp.arange(HEAD_SIZE // 2, dtype=f32) * 2.0) / HEAD_SIZE)
    angles = positions.astype(f32)[:, None] * frequency[None, :]
    cos, sin = jnp.cos(angles), jnp.sin(angles)
    return jnp.concatenate([cos] * 4, axis=1), jnp.concatenate([-sin, sin, -sin, sin], axis=1)


def plain_dot(left, right):
    return jnp.dot(left, right, preferred_element_type=f32)


def left_dot(left, right):
    return lax.dot_general(left, right, (((0,), (0,)), ((), ())), preferred_element_type=f32)


def right_dot(left, right):
    return lax.dot_general(left, right, (((1,), (1,)), ((), ())), preferred_element_type=f32)


def shift(block, axis, step, size=4):
    return lax.ppermute(block, axis, [(i, (i - step) % size) for i in range(size)])


def scatter_parts(blocks, axis):
    rows = blocks.shape[0] // 4
    parts = [blocks[k * rows : (k + 1) * rows] for k in range(4)]
    return [parts[0]] + [shift(parts[k], axis, -k) for k in (1, 2, 3)]


def add_parts(parts):
    total = parts[0].astype(f32)
    for part in parts[1:]:
        total = total + part.astype(f32)
    return total


def scatter_axis(blocks, axis):
    return add_parts(scatter_parts(blocks, axis)).astype(blocks.dtype)


def gather_blocks(block):
    blocks = [block] + [shift(block, "z", k) for k in (1, 2, 3)]
    return blocks, shift(jnp.concatenate(blocks, axis=0), "core", 1, 2)


def scatter_fsdp_parts(blocks):
    half = blocks.shape[0] // 2
    mine = blocks[:half].astype(f32) + shift(blocks[half:], "core", 1, 2).astype(f32)
    return scatter_parts(mine.astype(blocks.dtype), "z")


def gather_ordered(shard):
    z, core = lax.axis_index("z"), lax.axis_index("core")
    blocks, other = gather_blocks(shard[None])
    out = jnp.zeros((4, 2) + shard.shape, shard.dtype)
    for k in range(4):
        mine, its = blocks[k], other[k : k + 1]
        pair = jnp.concatenate([jnp.where(core == 0, mine, its), jnp.where(core == 0, its, mine)], axis=0)
        out = lax.dynamic_update_index_in_dim(out, pair, (z + k) % 4, 0)
    return out.reshape((8 * shard.shape[0],) + shard.shape[1:])


def scatter_ordered(partial):
    z, core = lax.axis_index("z"), lax.axis_index("core")
    own = partial.shape[0] // 8
    view = partial.reshape(4, 2, own, -1)
    mine = lax.dynamic_index_in_dim(view, core, 1, keepdims=False)
    its = lax.dynamic_index_in_dim(view, 1 - core, 1, keepdims=False)
    mine = (mine.astype(f32) + shift(its, "core", 1, 2).astype(f32)).astype(partial.dtype)
    pick = lambda k: lax.dynamic_index_in_dim(mine, (z + k) % 4, 0, keepdims=False)
    return add_parts([pick(0)] + [shift(pick(k), "z", -k) for k in (1, 2, 3)]).astype(partial.dtype)


def sum_ctx(value):
    x = lax.axis_index("x")
    pick = lambda k: lax.dynamic_index_in_dim(value, (x + k) % 4, 0, keepdims=False)
    low = add_parts([pick(0)] + [shift(pick(k), "x", -k) for k in (1, 2, 3)]).astype(value.dtype)
    low = add_parts([low] + [shift(low, "y", k) for k in (1, 2, 3)]).astype(value.dtype)
    out = jnp.zeros(value.shape, value.dtype)
    for k in range(4):
        out = lax.dynamic_update_index_in_dim(out, low if k == 0 else shift(low, "x", k), (x + k) % 4, 0)
    return out


def params(*semantics):
    return pltpu.CompilerParams(vmem_limit_bytes=56 * 2**20)


def cost(flops, read):
    return pl.CostEstimate(flops=int(flops), bytes_accessed=int(read), transcendentals=0)


def swap_halves(value):
    lane = lax.broadcasted_iota(jnp.int32, value.shape, 1)
    return jnp.where(lane % HEAD_SIZE < HEAD_SIZE // 2, pltpu.roll(value, 96, 1), pltpu.roll(value, 32, 1))


def rope(value, cos, sin):
    return value * cos + swap_halves(value) * sin


def rope_keys(value, cos, sin):
    chunks = []
    for j in range(5):
        part = value[:, j * 128 : (j + 1) * 128]
        if j < 2:
            part = rope(part, cos, sin)
        elif j == 2:
            lane = lax.broadcasted_iota(jnp.int32, part.shape, 1)
            part = jnp.where(lane < 64, rope(part, cos, sin), part)
        chunks.append(part)
    return chunks


def qkv_kernel(all_ref, cos_ref, sin_ref, own_ref, own_cos_ref, own_sin_ref, w_ref, gain_ref, ha_ref, kv_ref, q_ref):
    def normed(ref):
        rows = ref[...].astype(f32)
        inv = lax.rsqrt(jnp.mean(rows * rows, axis=1, keepdims=True) + EPSILON)
        return (rows * inv * gain_ref[...]).astype(bf16)

    ha = normed(all_ref)
    ha_ref[...] = ha
    kv = plain_dot(ha, w_ref[:, : 2 * KD])
    for j, part in enumerate(rope_keys(kv, cos_ref[...], sin_ref[...])):
        kv_ref[:, j * 128 : (j + 1) * 128] = part.astype(bf16)

    @pl.when(pl.program_id(0) == 0)
    def _():
        q = plain_dot(normed(own_ref), w_ref[:, 2 * KD :])
        for j in range(8):
            cols = slice(j * 128, (j + 1) * 128)
            part = rope(q[:, cols], own_cos_ref[...], own_sin_ref[...])
            q_ref[:, cols] = (part.astype(bf16).astype(f32) * HEAD_SIZE**-0.5).astype(bf16)


def qkv_call(rows_all, cos, sin, own, own_cos, own_sin, w, gain):
    length, width = rows_all.shape
    tile = 256
    whole = lambda a: pl.BlockSpec(a.shape, lambda i: (0, 0))
    tiled = lambda c: pl.BlockSpec((tile, c), lambda i: (i, 0))
    return pl.pallas_call(
        qkv_kernel,
        grid=(length // tile,),
        in_specs=[tiled(width), tiled(128), tiled(128)] + [whole(a) for a in (own, own_cos, own_sin, w, gain)],
        out_specs=[tiled(width), tiled(2 * KD), pl.BlockSpec((own.shape[0], 1024), lambda i: (0, 0))],
        out_shape=[
            jax.ShapeDtypeStruct((length, width), bf16),
            jax.ShapeDtypeStruct((length, 2 * KD), bf16),
            jax.ShapeDtypeStruct((own.shape[0], 1024), bf16),
        ],
        compiler_params=params(),
        cost_estimate=cost(3e9, 12e6),
        name="qkv",
    )(rows_all, cos, sin, own, own_cos, own_sin, w, gain)


def attend_kernel(
    q_ref, kv_ref, qpos_ref, qdoc_ref, kpos_ref, kdoc_ref, x_ref, w_ref, gain_ref,
    o_ref, lse_ref, mid_ref, hm_ref, qs, ks, vs, os, bias,
):
    rows = x_ref.shape[0]
    for n in range(QUERY_HEADS):
        qs[n] = q_ref[:, n * 64 : (n + 1) * 64]
    for n in range(KEY_VALUE_HEADS):
        ks[n] = kv_ref[:, n * 64 : (n + 1) * 64]
        vs[n] = kv_ref[:, KD + n * 64 : KD + (n + 1) * 64]
    ok = (qdoc_ref[...] == kdoc_ref[...]) & (qpos_ref[...] >= kpos_ref[...])
    bias[...] = jnp.where(ok, 0.0, NEGATIVE)

    def head(h, carry):
        for g in range(GROUP):
            n = h * GROUP + g
            s = right_dot(qs[n], ks[h]) + bias[...]
            top = jnp.max(s, axis=1, keepdims=True)
            p = jnp.exp(s - top)
            total = jnp.sum(p, axis=1, keepdims=True)
            o = plain_dot((p * (1.0 / total)).astype(bf16), vs[h])
            os[n] = o.astype(bf16)
            lse = jnp.broadcast_to(top + jnp.log(total), (rows, rows))
            lse_ref[pl.ds(n, 1), :] = jnp.transpose(lse)[:1, :]
        return carry

    lax.fori_loop(0, KEY_VALUE_HEADS, head, 0)
    for n in range(QUERY_HEADS):
        o_ref[:, n * 64 : (n + 1) * 64] = os[n]
    mid = x_ref[...].astype(f32) + plain_dot(o_ref[...], w_ref[...])
    mid_ref[...] = mid
    inv = lax.rsqrt(jnp.mean(mid * mid, axis=1, keepdims=True) + EPSILON)
    hm_ref[...] = (mid * inv * gain_ref[...]).astype(bf16)


def attend_call(q, kv, qpos, qdoc, kpos, kdoc, x, w, gain):
    rows, width = x.shape
    length = kv.shape[0]
    return pl.pallas_call(
        attend_kernel,
        out_shape=[
            jax.ShapeDtypeStruct((rows, width), bf16),
            jax.ShapeDtypeStruct((16, rows), f32),
            jax.ShapeDtypeStruct((rows, width), f32),
            jax.ShapeDtypeStruct((rows, width), bf16),
        ],
        scratch_shapes=[
            pltpu.VMEM((QUERY_HEADS, rows, 64), bf16),
            pltpu.VMEM((KEY_VALUE_HEADS, length, 64), bf16),
            pltpu.VMEM((KEY_VALUE_HEADS, length, 64), bf16),
            pltpu.VMEM((QUERY_HEADS, rows, 64), bf16),
            pltpu.VMEM((rows, length), f32),
        ],
        compiler_params=params(),
        cost_estimate=cost(5e9, 8e6),
        name="attend",
    )(q, kv, qpos, qdoc, kpos, kdoc, x, w, gain)


def mlp_kernel(h0, h1, h2, h3, ho, dy_ref, wg_ref, wu_ref, wd_ref, all_ref, act_ref, dg_ref, du_ref, dh_ref, out_ref):
    rows = h0.shape[0]
    for k, ref in enumerate((h0, h1, h2, h3)):
        all_ref[k * rows : (k + 1) * rows, :] = ref[...]
    all_ref[4 * rows :, :] = ho[...]

    def tile(t, carry):
        at = pl.ds(pl.multiple_of(t * 256, 256), 256)
        h, dy = all_ref[at, :], dy_ref[at, :]
        gate = plain_dot(h, wg_ref[...])
        up = plain_dot(h, wu_ref[...])
        d_act = right_dot(dy, wd_ref[...])
        sig = jax.nn.sigmoid(gate)
        act = (gate * sig * up).astype(bf16)
        dg = (d_act * up * sig * (1.0 + gate * (1.0 - sig))).astype(bf16)
        du = (d_act * gate * sig).astype(bf16)
        act_ref[at, :] = act
        dg_ref[at, :] = dg
        du_ref[at, :] = du
        dh_ref[at, :] = (right_dot(dg, wg_ref[...]) + right_dot(du, wu_ref[...])).astype(bf16)
        out_ref[at, :] = plain_dot(act, wd_ref[...]).astype(bf16)
        return carry

    lax.fori_loop(0, all_ref.shape[0] // 256, tile, 0)


def mlp_call(blocks, other, dy, wg, wu, wd):
    total, width = dy.shape
    ff = wg.shape[1]
    wide, slim = jax.ShapeDtypeStruct((total, width), bf16), jax.ShapeDtypeStruct((total, ff), bf16)
    return pl.pallas_call(
        mlp_kernel,
        out_shape=[wide, slim, slim, slim, wide, wide],
        compiler_params=params(),
        cost_estimate=cost(4e9, 12e6),
        name="mlp",
    )(*blocks, other, dy, wg, wu, wd)


def norm_back(grad_normed, normed, inv_rms, gain):
    scaled = grad_normed * gain
    return inv_rms * (scaled - normed * jnp.mean(scaled * normed, axis=1, keepdims=True))


def middle_kernel(d0, d1, d2, d3, dy_ref, mid_ref, gain_ref, w_ref, o_ref, dmid_ref, low_ref, do_ref, delta_ref):
    rows = mid_ref.shape[0]
    d_hm = add_parts([d0[...], d1[...], d2[...], d3[...]])
    mid = mid_ref[...]
    inv = lax.rsqrt(jnp.mean(mid * mid, axis=1, keepdims=True) + EPSILON)
    d_mid = dy_ref[...].astype(f32) + norm_back(d_hm, mid * inv, inv, gain_ref[...])
    dmid_ref[...] = d_mid
    low = d_mid.astype(bf16)
    low_ref[...] = low
    d_o = right_dot(low, w_ref[...]).astype(bf16)
    do_ref[...] = d_o
    prod = d_o.astype(f32) * o_ref[...].astype(f32)
    for n in range(QUERY_HEADS):
        one = jnp.sum(prod[:, n * 64 : (n + 1) * 64], axis=1, keepdims=True)
        delta_ref[n : n + 1, :] = jnp.transpose(jnp.broadcast_to(one, (rows, rows)))[:1, :]


def middle_call(parts, dy, mid, gain, w, o):
    rows, width = mid.shape
    wide = lambda t: jax.ShapeDtypeStruct((rows, width), t)
    return pl.pallas_call(
        middle_kernel,
        out_shape=[wide(f32), wide(bf16), wide(bf16), jax.ShapeDtypeStruct((16, rows), f32)],
        compiler_params=params(),
        cost_estimate=cost(1e9, 4e6),
        name="middle",
    )(*parts, dy, mid, gain, w, o)


def back_kernel(
    q_ref, kv_ref, do_ref, lse_ref, delta_ref, qpos_ref, qdoc_ref, kpos_ref, kdoc_ref,
    cos_ref, sin_ref, own_cos_ref, own_sin_ref, dq_ref, dkv_ref, qs, ds, ks, vs, dks, dvs, dqs, bias,
):
    rows, length = do_ref.shape[0], kv_ref.shape[0]
    chunk = 512
    for n in range(QUERY_HEADS):
        h, g = n // GROUP, n % GROUP
        qs[h, g * rows : (g + 1) * rows, :] = q_ref[:, n * 64 : (n + 1) * 64]
        ds[h, g * rows : (g + 1) * rows, :] = do_ref[:, n * 64 : (n + 1) * 64]
    for n in range(KEY_VALUE_HEADS):
        ks[n] = kv_ref[:, n * 64 : (n + 1) * 64]
        vs[n] = kv_ref[:, KD + n * 64 : KD + (n + 1) * 64]
    ok = (kdoc_ref[...] == qdoc_ref[...]) & (qpos_ref[...] >= kpos_ref[...])
    bias[...] = jnp.where(ok, 0.0, NEGATIVE)

    def head(h, carry):
        q, d = qs[h], ds[h]
        row = lambda ref: jnp.concatenate([ref[pl.ds(h * GROUP + g, 1), :] for g in range(GROUP)], axis=1)
        lse, delta = row(lse_ref), row(delta_ref)

        def step(c, dq):
            at = pl.ds(pl.multiple_of(c * chunk, chunk), chunk)
            k, v = ks[h, at, :], vs[h, at, :]
            b = bias[at, :]
            p = jnp.exp(right_dot(k, q) + jnp.concatenate([b, b, b], axis=1) - lse)
            dp = right_dot(v, d)
            low = p.astype(bf16)
            dscore = (p * (dp - delta)).astype(bf16)
            dvs[h, at, :] = plain_dot(low, d)
            dks[h, at, :] = plain_dot(dscore, q)
            return dq + left_dot(k, dscore)

        dqs[h] = lax.fori_loop(0, length // chunk, step, jnp.zeros((64, GROUP * rows), f32))
        return carry

    lax.fori_loop(0, KEY_VALUE_HEADS, head, 0)
    own_cos, own_sin = own_cos_ref[...], -own_sin_ref[...]
    scale = HEAD_SIZE**-0.5
    for j in range(8):
        pieces = []
        for n in (2 * j, 2 * j + 1):
            n = min(n, QUERY_HEADS - 1)
            pieces.append(dqs[n // GROUP, :, (n % GROUP) * rows : (n % GROUP + 1) * rows])
        part = jnp.transpose(jnp.concatenate(pieces, axis=0)) * scale
        dq_ref[:, j * 128 : (j + 1) * 128] = rope(part, own_cos, own_sin).astype(bf16)

    def finish(t, carry):
        at = pl.ds(pl.multiple_of(t * 256, 256), 256)
        parts = [dks[n, at, :] for n in range(KEY_VALUE_HEADS)] + [dvs[n, at, :] for n in range(KEY_VALUE_HEADS)]
        both = jnp.concatenate(parts, axis=1)
        for j, part in enumerate(rope_keys(both, cos_ref[at, :], -sin_ref[at, :])):
            dkv_ref[at, j * 128 : (j + 1) * 128] = part.astype(bf16)
        return carry

    lax.fori_loop(0, length // 256, finish, 0)


def back_call(q, kv, d_o, lse, delta, qpos, qdoc, kpos, kdoc, cos, sin, own_cos, own_sin):
    rows, length = d_o.shape[0], kv.shape[0]
    both = GROUP * rows
    return pl.pallas_call(
        back_kernel,
        out_shape=[jax.ShapeDtypeStruct((rows, 1024), bf16), jax.ShapeDtypeStruct((length, 2 * KD), bf16)],
        scratch_shapes=[
            pltpu.VMEM((KEY_VALUE_HEADS, both, 64), bf16),
            pltpu.VMEM((KEY_VALUE_HEADS, both, 64), bf16),
            pltpu.VMEM((KEY_VALUE_HEADS, length, 64), bf16),
            pltpu.VMEM((KEY_VALUE_HEADS, length, 64), bf16),
            pltpu.VMEM((KEY_VALUE_HEADS, length, 64), f32),
            pltpu.VMEM((KEY_VALUE_HEADS, length, 64), f32),
            pltpu.VMEM((KEY_VALUE_HEADS, 64, both), f32),
            pltpu.VMEM((length, rows), f32),
        ],
        compiler_params=params(),
        cost_estimate=cost(20e9, 8e6),
        name="back",
    )(q, kv, d_o, lse, delta, qpos, qdoc, kpos, kdoc, cos, sin, own_cos, own_sin)


def last_kernel(dq_ref, dkv_ref, w_ref, x_ref, gain_ref, dmid_ref, out_ref):
    d_ha = right_dot(dkv_ref[...], w_ref[:, : 2 * KD]) + right_dot(dq_ref[:, :QD], w_ref[:, 2 * KD : 2 * KD + QD])
    x = x_ref[...].astype(f32)
    inv = lax.rsqrt(jnp.mean(x * x, axis=1, keepdims=True) + EPSILON)
    out_ref[...] = (dmid_ref[...] + norm_back(d_ha, x * inv, inv, gain_ref[...])).astype(bf16)


def last_call(dq, dkv, w, x, gain, d_mid):
    return pl.pallas_call(
        last_kernel,
        out_shape=jax.ShapeDtypeStruct(x.shape, bf16),
        compiler_params=params(),
        cost_estimate=cost(1e9, 5e6),
        name="last",
    )(dq, dkv, w, x, gain, d_mid)


def per_device(
    hidden,
    cotangent,
    pairing,
    documents,
    attn_gain,
    w_query,
    w_key,
    w_value,
    w_out,
    mlp_gain,
    w_gate,
    w_up,
    w_down,
):
    rows, width = hidden.shape[2:]
    half = rows // 2
    own = width // 8
    ff = w_gate.shape[1] // 8
    me = lax.axis_index("x") * 4 + lax.axis_index("y")
    x_rows = hidden.reshape(rows, width)
    dy = cotangent.reshape(rows, width)

    rows_all = lax.all_gather(x_rows, CTX, axis=0, tiled=True)
    shard = jnp.concatenate(
        [w_key, w_value, w_query, attn_gain[:, None], mlp_gain[:, None], jnp.zeros((own, PADDED - 2 * KD - QD - 2), bf16), w_out],
        axis=1,
    )
    weights = gather_ordered(shard)
    dy_blocks, dy_other = gather_blocks(dy)
    dy_all = jnp.concatenate(dy_blocks + [dy_other], axis=0)
    gate_up = jnp.concatenate([w_gate.reshape(own, 8, ff), w_up.reshape(own, 8, ff)], axis=2).transpose(1, 0, 2)
    gate_up = lax.all_to_all(gate_up, FSDP, 0, 0, tiled=True).reshape(width, 2 * ff)
    rows_all, weights, dy_all, gate_up = lax.optimization_barrier((rows_all, weights, dy_all, gate_up))
    w_kvq, out_w = weights[:, :PADDED], weights[:, PADDED:]
    gains = weights[:, PADDED - 64 : PADDED - 62].astype(f32).T
    gain_a, gain_m = gains[:1], gains[1:]
    wg, wu = gate_up[:, :ff], gate_up[:, ff:]

    positions = seq_positions(pairing, rows)
    docs = documents[:, 0, :]
    cos, sin = rope_tables(positions.reshape(-1))
    own_cos = lax.dynamic_slice_in_dim(cos, me * rows, rows, 0)
    own_sin = lax.dynamic_slice_in_dim(sin, me * rows, rows, 0)
    own_pos = lax.dynamic_index_in_dim(positions, me, 0)
    own_doc = lax.dynamic_index_in_dim(docs, me, 0)

    ha_all, kv, q = qkv_call(rows_all, cos, sin, x_rows, own_cos, own_sin, w_kvq, gain_a)
    o, lse, mid, hm = attend_call(
        q, kv, own_pos.reshape(-1, 1), own_doc.reshape(-1, 1), positions.reshape(1, -1), docs.reshape(1, -1), x_rows, out_w, gain_m
    )

    hm_blocks, hm_other = gather_blocks(hm)
    h_all, act, dg, du, dh_part, out_part = mlp_call(hm_blocks, hm_other, dy_all, wg, wu, w_down)
    dh_parts = scatter_fsdp_parts(dh_part)
    d_mid, low, d_o, delta = middle_call(dh_parts, dy, mid, gain_m, out_w, o)
    result = (mid + add_parts(scatter_fsdp_parts(out_part))).astype(bf16)

    g_gate, g_up = left_dot(h_all, dg).astype(bf16), left_dot(h_all, du).astype(bf16)
    g_gu = jnp.concatenate([g_gate.reshape(8, own, ff), g_up.reshape(8, own, ff)], axis=2)
    g_gu = lax.all_to_all(g_gu, FSDP, 0, 0, tiled=True)
    g_down = left_dot(act, dy_all).astype(bf16)
    g_gu, g_down = lax.psum((g_gu, g_down), CTX)
    g_gu = g_gu.astype(f32)
    g_gate = g_gu[:, :, :ff].transpose(1, 0, 2).reshape(own, -1)
    g_up = g_gu[:, :, ff:].transpose(1, 0, 2).reshape(own, -1)
    g_gain_m = (jnp.sum(g_gate * w_gate, axis=1) + jnp.sum(g_up * w_up, axis=1)) / mlp_gain.astype(f32)

    g_out = scatter_ordered(left_dot(o, low).astype(bf16))

    dq, dkv = back_call(
        q, kv, d_o, lse, delta, own_pos, own_doc, positions.reshape(-1, 1), docs.reshape(-1, 1), cos, sin, own_cos, own_sin
    )
    ha_own = lax.dynamic_slice_in_dim(ha_all, me * rows, rows, 0)
    g_kvq = jnp.concatenate([left_dot(ha_all, dkv), left_dot(ha_own, dq[:, :QD])], axis=1).astype(bf16)
    g_kvq = scatter_ordered(g_kvq)
    total = jnp.concatenate([g_kvq, g_out], axis=1)
    total = sum_ctx(total.reshape(4, own // 4, -1)).reshape(own, -1).astype(f32)
    g_key, g_value, g_query = total[:, :KD], total[:, KD : 2 * KD], total[:, 2 * KD : 2 * KD + QD]
    g_out = total[:, 2 * KD + QD :]
    g_gain_a = (
        jnp.sum(g_key * w_key, axis=1) + jnp.sum(g_value * w_value, axis=1) + jnp.sum(g_query * w_query, axis=1)
    ) / attn_gain.astype(f32)

    x, y = lax.axis_index("x"), lax.axis_index("y")

    def to_owners(part, first, second, i, j):
        view = part.reshape(4, 4 * half, -1)
        pick = lambda k: lax.dynamic_index_in_dim(view, (i + k) % 4, 0, keepdims=False)
        part = add_parts([pick(0)] + [shift(pick(k), first, -k) for k in (1, 2, 3)]).astype(bf16)
        view = part.reshape(4, half, -1)
        return add_parts(
            [lax.dynamic_index_in_dim(view, j, 0, keepdims=False)]
            + [shift(lax.dynamic_index_in_dim(view, (j + k) % 4, 0, keepdims=False), second, -k) for k in (1, 2, 3)]
        ).astype(bf16)

    blocks = dkv.reshape(4, 4, 2, half, 2 * KD)
    early = to_owners(blocks[:, :, 0], "x", "y", x, y)
    late = to_owners(blocks[:, :, 1].swapaxes(0, 1), "y", "x", y, x)
    input_grad = last_call(dq, jnp.concatenate([early, late], axis=0), w_kvq, x_rows, gain_a, d_mid)

    return (
        result.reshape(1, 1, rows, width),
        input_grad.reshape(1, 1, rows, width),
        g_gain_a,
        g_query,
        g_key,
        g_value,
        g_out,
        g_gain_m,
        g_gate,
        g_up,
        g_down.astype(f32),
    )


def solution(mesh):
    grid = jax.sharding.Mesh(mesh.devices.reshape(4, 4, 4, 2), ("x", "y", "z", "core"))
    tokens = P(CTX, FSDP, None, None)
    vector, matrix = P(FSDP), P(FSDP, None)
    return jax.shard_map(
        per_device,
        mesh=grid,
        in_specs=(tokens, tokens, P(), P(None, FSDP, None), vector, matrix, matrix, matrix, matrix, vector, matrix, matrix, matrix),
        out_specs=(tokens, tokens, vector, matrix, matrix, matrix, matrix, vector, matrix, matrix, matrix),
        check_vma=False,
    )
```

time: 917 us -> 433 us (0.47)
  waiting for transfers between devices: 615 us -> 95 us
  matrix products: 145 us -> 15.1 us
  blocking collectives: 94.7 us -> 0 us
  starting transfers between devices: 1.09 us -> 80.1 us
  Pallas kernels: 0 us -> 75 us
  local copies, waits for them, and re-layouts: 24 us -> 90.6 us
  other arithmetic: 18.1 us -> 54 us
    all_gather x7 -> x1, waiting for transfers between devices: 197 us -> 0.01 us  [per_device(): rows_all = lax.all_gather(x_rows, CTX, axis=0, tiled=True)]
    unnamed x19 -> x2, waiting for transfers between devices: 191 us -> 0.03 us
    reduce_scatter x5 -> x0, waiting for transfers between devices: 190 us -> none  [the longest x1 41.6 us: per_device(): lax.psum_scatter(grad_down.astype(jnp.bfloat16), 'fsdp', scatter_dimensio...]
    ppermute x0 -> x49, waiting for transfers between devices: none -> 94.9 us  [shift(): lax.ppermute(block, axis, [(i, (i - step) % size) for i in range(size)])]
    dot_general x34 -> x0, matrix products: 80.8 us -> none  [the longest x17 42.7 us: right_dot(): lax.dot_general(left, right, (((1,), (1,)), ((), ())), preferred_element_...]
    pallas_call x0 -> x6, Pallas kernels: none -> 75 us  [the longest x1 24.1 us: back_call(): pl.pallas_call(back_kernel, out_shape=[jax.ShapeDtypeStruct((rows, 1024),...]
    ppermute x0 -> x49, starting transfers between devices: none -> 68.4 us  [shift(): lax.ppermute(block, axis, [(i, (i - step) % size) for i in range(size)])]
    psum x1 -> x0, blocking collectives: 40.4 us -> none  [per_device(): lax.psum(gain_a_sum.astype(jnp.bfloat16), 'ctx').astype(jnp.float32)]
  transfers between devices with their start and end apart: 16 -> 53, of which waited for: 16 -> 23; matrix products, arithmetic and copies ran while one was open for 8% -> 28% of each run, Pallas kernels for 0% -> 8%
where the time goes in v1:
time: 433 us; the launch traced here: 425 us
  waiting for transfers between devices  95 us (22%)
  local copies, waits for them, and re-layouts  90.6 us (21%)
  starting transfers between devices  80.1 us (18%)
  Pallas kernels  75 us (17%)
  other arithmetic  54 us (12%)
  matrix products  15.1 us (3%)
  between operations  15 us (3%)
    ppermute x49, waiting for transfers between devices, shift(): lax.ppermute(block, axis, [(i, (i - step) % size) for i in range(size)])  94.9 us
    ppermute x49, starting transfers between devices, shift(): lax.ppermute(block, axis, [(i, (i - step) % size) for i in range(size)])  68.4 us
    pallas_call x1, Pallas kernels, back_call(): pl.pallas_call(back_kernel, out_shape=[jax.ShapeDtypeStruct((rows, 1024),...  24.1 us
    unnamed x88, local copies, waits for them, and re-layouts  21.1 us
    pallas_call x1, Pallas kernels, attend_call(): pl.pallas_call(attend_kernel, out_shape=[jax.ShapeDtypeStruct((rows, widt...  17.3 us
    dot_general x6, matrix products, left_dot(): lax.dot_general(left, right, (((0,), (0,)), ((), ())), preferred_element_...  15.1 us
    pallas_call x1, Pallas kernels, mlp_call(): pl.pallas_call(mlp_kernel, out_shape=[wide, slim, slim, slim, wide, wide]...  12.4 us
    pallas_call x1, Pallas kernels, qkv_call(): pl.pallas_call(qkv_kernel, grid=(length // tile,), in_specs=[tiled(width)...  12.3 us
  transfers between devices with their start and end apart: 53, of which 23 were waited for; matrix products, arithmetic and copies ran while one was open for 28% of the time, Pallas kernels for 8%

profile of v1, /device:TPU:32, one launch (start us, length us, event | category | flops | bytes accessed | tf_op | source)
XLA Modules:
  0.0 424.8 jit_solution(8181380655603976103)
XLA Ops:
  14.5 3.4 collective-permute-start.1
  27.3 6.1 %all-to-all-start = ((bf16[8,120,640]{2,1,0:T(8,128)(2,1)}), bf16[8,120,640]{2,1,0:T(8,128)(2,1)S(1)}, u32[]{:S(2)}, u32[]{:S(2)}) async-start(bf16[8,120,640]{2,1,0:T(8,128)(2,1)} %copy.135), calls=%async_computation | async-start | bytes 2457600 | tf_op jit(solution)/shard_map/all_to_all | solution.py:452
  35.0 12.2 %collective-permute-done.1 = bf16[1,120,2624]{2,1,0:T(8,128)(2,1)} collective-permute-done((bf16[1,120,2624]{2,1,0:T(8,128)(2,1)S(1)}, bf16[1,120,2624]{2,1,0:T(8,128)(2,1)}, u32[]{:S(2)}, u32[]{:S(2)}) %collective-permute-start.1) | collective-permute-done | bytes 629792 | tf_op jit(solution)/shard_map/ppermute | solution.py:55
  48.0 3.5 pad_maximum_fusion
  51.6 5.7 %fusion.22 = (f32[2048,32]{1,0:T(8,128)}, f32[2048,32]{1,0:T(8,128)}, f32[2048,32]{1,0:T(8,128)}) fusion(f32[32]{0:T(128)S(1)} %multiply_power_fusion, f32[2048]{0:T(1024)S(1)} %get-tuple-element.168), kind=kLoop, calls=%fused_computation.73 | loop fusion | flops 131072 | bytes 794752 | tf_op jit(solution)/shard_map/neg | solution.py:39
  59.9 11.4 %collective-permute-done.6 = bf16[128,960]{1,0:T(8,128)(2,1)} collective-permute-done((bf16[128,960]{1,0:T(8,128)(2,1)S(1)}, bf16[128,960]{1,0:T(8,128)(2,1)}, u32[]{:S(2)}, u32[]{:S(2)}) %collective-permute-start.6) | collective-permute-done | bytes 245792 | tf_op jit(solution)/shard_map/ppermute | solution.py:55
  76.2 5.5 %pad_maximum_fusion.3 = (f32[2048,128]{1,0:T(8,128)S(1)}, f32[2048,128]{1,0:T(8,128)S(1)}) fusion(f32[2048,32]{1,0:T(8,128)} %get-tuple-element.162, f32[2048,32]{1,0:T(8,128)} %get-tuple-element.161, f32[2048,32]{1,0:T(8,128)} %get-tuple-element.160), kind=kLoop, calls=%fused_computation.39 | loop fusion | flops 1572864 | bytes 2883584 | tf_op jit(solution)/shard_map/concatenate | solution.py:39
  101.5 8.1 %copy.138 = bf16[960,2624]{0,1:T(8,128)(2,1)} copy(bf16[960,2624]{1,0:T(8,128)(2,1)} %bitcast.8) | data formatting | bytes 10076160 | tf_op jit(solution)/shard_map/optimization_barrier | solution.py:453
  109.6 3.8 slice.100.w_ref
  117.7 12.3 %qkv.1 = (bf16[2048,960]{1,0:T(8,128)(2,1)}, bf16[2048,640]{1,0:T(8,128)(2,1)}, bf16[128,1024]{1,0:T(8,128)(2,1)}) custom-call(bf16[2048,960]{1,0:T(8,128)(2,1)} %bitcast.210, f32[2048,128]{1,0:T(8,128)} %copy-done.11, f32[2048,128]{1,0:T(8,128)} %copy-done.12, bf16[128,960]{1,0:T(8,128)(2,1)} %bitcast.196, ...), custom_call_target="tpu_custom_call" | custom-call | flops 3000000000 | bytes 12000000 | tf_op jit(solution)/shard_map/qkv/pallas_call | solution.py:175
  130.0 17.3 %attend.1 = (bf16[128,960]{1,0:T(8,128)(2,1)}, f32[16,128]{1,0:T(8,128)}, f32[128,960]{1,0:T(8,128)}, bf16[128,960]{1,0:T(8,128)(2,1)}) custom-call(bf16[128,1024]{1,0:T(8,128)(2,1)} %get-tuple-element.36.q_ref, bf16[2048,640]{1,0:T(8,128)(2,1)} %get-tuple-element.37.kv_ref, s32[128,1]{1,0:T(8,128)} %copy.139.qpos_ref, s32[128,1]{1,0:T(8,128)} %copy.140.qdoc_ref, ...), custom_call_target="tpu_custom_call" | custom-call | flops 5000000000 | bytes 8000000 | tf_op jit(solution)/shard_map/attend/pallas_call | solution.py:229
  152.2 5.3 %collective-permute-done.10.h3 = bf16[128,960]{1,0:T(8,128)(2,1)S(1)} collective-permute-done((bf16[128,960]{1,0:T(8,128)(2,1)}, bf16[128,960]{1,0:T(8,128)(2,1)S(1)}, u32[]{:S(2)}, u32[]{:S(2)}) %collective-permute-start.10) | collective-permute-done | bytes 245792 | tf_op jit(solution)/shard_map/ppermute | solution.py:55
  157.5 7.2 %collective-permute-done.9.h2 = bf16[128,960]{1,0:T(8,128)(2,1)S(1)} collective-permute-done((bf16[128,960]{1,0:T(8,128)(2,1)}, bf16[128,960]{1,0:T(8,128)(2,1)S(1)}, u32[]{:S(2)}, u32[]{:S(2)}) %collective-permute-start.9) | collective-permute-done | bytes 245792 | tf_op jit(solution)/shard_map/ppermute | solution.py:55
  174.1 12.4 %mlp.1 = (bf16[1024,960]{1,0:T(8,128)(2,1)}, bf16[1024,320]{1,0:T(8,128)(2,1)}, bf16[1024,320]{1,0:T(8,128)(2,1)}, bf16[1024,320]{1,0:T(8,128)(2,1)}, bf16[1024,...) custom-call(bf16[128,960]{1,0:T(8,128)(2,1)} %get-tuple-element.39.h0, bf16[128,960]{1,0:T(8,128)(2,1)} %copy-done.26, ...), custom_call_target="tpu_custom_call" | custom-call | flops 4000000000 | bytes 12000000 | tf_op jit(solution)/shard_map/mlp/pallas_call | solution.py:280
  199.7 5.5 %all-to-all-start.1 = ((bf16[8,120,640]{2,1,0:T(8,128)(2,1)}), bf16[8,120,640]{2,1,0:T(8,128)(2,1)S(1)}, u32[]{:S(2)}, u32[]{:S(2)}) async-start(bf16[8,120,640]{2,1,0:T(8,128)(2,1)} %pad_maximum_fusion.1), calls=%async_computation.1 | async-start | bytes 2457600 | tf_op jit(solution)/shard_map/all_to_all | solution.py:480
  205.3 3.3 convolution_convert_fusion.3
  223.7 3.5 collective-permute-start.14
  228.8 4.8 %collective-permute-done.19.d3 = bf16[128,960]{1,0:T(8,128)(2,1)} collective-permute-done((bf16[128,960]{1,0:T(8,128)(2,1)}, bf16[128,960]{1,0:T(8,128)(2,1)}, u32[]{:S(2)}, u32[]{:S(2)}) %collective-permute-start.19) | collective-permute-done | bytes 245792 | tf_op jit(solution)/shard_map/ppermute | solution.py:55
  233.6 4.8 %middle.1 = (f32[128,960]{1,0:T(8,128)}, bf16[128,960]{1,0:T(8,128)(2,1)}, bf16[128,960]{1,0:T(8,128)(2,1)}, f32[16,128]{1,0:T(8,128)}) custom-call(bf16[128,960]{1,0:T(8,128)(2,1)} %get-tuple-element.144.d0, bf16[128,960]{1,0:T(8,128)(2,1)} %copy-done.23, bf16[128,960]{1,0:T(8,128)(2,1)} %collective-permute-done.18.d2, ...), custom_call_target="tpu_custom_call" | custom-call | flops 1000000000 | bytes 4000000 | tf_op jit(solution)/shard_map/middle/pallas_call | solution.py:314
  238.4 24.1 %back.1 = (bf16[128,1024]{1,0:T(8,128)(2,1)}, bf16[2048,640]{1,0:T(8,128)(2,1)}) custom-call(bf16[128,1024]{1,0:T(8,128)(2,1)} %get-tuple-element.36.q_ref, bf16[2048,640]{1,0:T(8,128)(2,1)} %get-tuple-element.37.kv_ref, bf16[128,960]{1,0:T(8,128)(2,1)} %get-tuple-element.45.do_ref, f32[16,128]{1,0:T(8,128)} %get-tuple-element.46.lse_ref, ...), custom_call_target="tpu_custom_call" | custom-call | flops 20000000000 | bytes 8000000 | tf_op jit(solution)/shard_map/back/pallas_call | solution.py:384
  262.5 5.1 %convolution_convert_fusion.2 = bf16[960,640]{1,0:T(8,128)(2,1)S(1)} fusion(bf16[2048,960]{1,0:T(8,128)(2,1)S(1)} %copy-done.31, bf16[2048,640]{1,0:T(8,128)(2,1)} %get-tuple-element.49), kind=kOutput, calls=%fused_computation.17 | convolution fusion | flops 2517196800 | bytes 7782400 | tf_op jit(solution)/shard_map/dot_general | solution.py:47
  289.2 7.7 %collective-permute-done.21 = bf16[256,640]{1,0:T(8,128)(2,1)} collective-permute-done((bf16[256,640]{1,0:T(8,128)(2,1)}, bf16[256,640]{1,0:T(8,128)(2,1)}, u32[]{:S(2)}, u32[]{:S(2)}) %collective-permute-start.21) | collective-permute-done | bytes 327712 | tf_op jit(solution)/shard_map/ppermute | solution.py:55
  296.9 3.1 collective-permute-start.27
  303.6 4.4 %collective-permute-done.27 = bf16[256,640]{1,0:T(8,128)(2,1)S(1)} collective-permute-done((bf16[256,640]{1,0:T(8,128)(2,1)S(1)}, bf16[256,640]{1,0:T(8,128)(2,1)S(1)}, u32[]{:S(2)}, u32[]{:S(2)}) %collective-permute-start.27) | collective-permute-done | bytes 327712 | tf_op jit(solution)/shard_map/ppermute | solution.py:55
  308.0 3.2 collective-permute-start.24
  311.2 9.2 %collective-permute-done.28 = bf16[256,640]{1,0:T(8,128)(2,1)S(1)} collective-permute-done((bf16[256,640]{1,0:T(8,128)(2,1)S(1)}, bf16[256,640]{1,0:T(8,128)(2,1)S(1)}, u32[]{:S(2)}, u32[]{:S(2)}) %collective-permute-start.28) | collective-permute-done | bytes 327712 | tf_op jit(solution)/shard_map/ppermute | solution.py:55
  327.5 3.6 collective-permute-done.29
  332.4 4.2 last.1
  340.5 5.1 %collective-permute-start.38 = (bf16[120,960]{1,0:T(8,128)(2,1)S(1)}, bf16[120,960]{1,0:T(8,128)(2,1)S(1)}, u32[]{:S(2)}, u32[]{:S(2)}) collective-permute-start(bf16[120,960]{1,0:T(8,128)(2,1)S(1)} %get-tuple-element.150), channel_id=1, source_target_pairs={{0,4},{2,6},{4,0},{6,2},{1,5},{3,7},{5,1},{7,3},{8,12},{10,14},{12... | collective-permute-start | bytes 691208 | tf_op jit(solution)/shard_map/ppermute | solution.py:55
  352.9 5.2 %collective-permute-start.35 = (bf16[120,1600]{1,0:T(8,128)(2,1)}, bf16[120,1600]{1,0:T(8,128)(2,1)}, u32[]{:S(2)}, u32[]{:S(2)}) collective-permute-start(bf16[120,1600]{1,0:T(8,128)(2,1)} %get-tuple-element.128), channel_id=1, source_target_pairs={{0,6},{2,0},{4,2},{6,4},{1,7},{3,1},{5,3},{7,5},{8,14},{10,8},{12,... | collective-permute-start | bytes 1152008 | tf_op jit(solution)/shard_map/ppermute | solution.py:55
  358.1 5.2 %collective-permute-done.39 = bf16[120,960]{1,0:T(8,128)(2,1)S(1)} collective-permute-done((bf16[120,960]{1,0:T(8,128)(2,1)S(1)}, bf16[120,960]{1,0:T(8,128)(2,1)S(1)}, u32[]{:S(2)}, u32[]{:S(2)}) %collective-permute-start.39) | collective-permute-done | bytes 230432 | tf_op jit(solution)/shard_map/ppermute | solution.py:55
  406.3 3.2 collective-permute-done.46
  (271 shorter events, 190.3 us)
Async XLA Ops:
  7.2 94.3 %all-gather.3.cloned.1.call-start = ((), (), s32[]{:S(2)}) async-start(), calls=%async_computation.2 | async-start | bytes 4456448 | tf_op jit(solution)/shard_map/all_gather | solution.py:443
  14.4 19.0 %collective-permute-start = (bf16[1,120,2624]{2,1,0:T(8,128)(2,1)S(1)}, bf16[1,120,2624]{2,1,0:T(8,128)(2,1)}, u32[]{:S(2)}, u32[]{:S(2)}) collective-permute-start(bf16[1,120,2624]{2,1,0:T(8,128)(2,1)S(1)} %bitcast.178), channel_id=1, source_target_pairs={{0,6},{2,0},{4,2},{6,4},{1,7},{3,1},{5,3},{7,5},{8,14},{10,8},{12,... | collective-permute-start | bytes 1889288 | tf_op jit(solution)/shard_map/ppermute | solution.py:55
  14.5 32.7 %collective-permute-start.1 = (bf16[1,120,2624]{2,1,0:T(8,128)(2,1)S(1)}, bf16[1,120,2624]{2,1,0:T(8,128)(2,1)}, u32[]{:S(2)}, u32[]{:S(2)}) collective-permute-start(bf16[1,120,2624]{2,1,0:T(8,128)(2,1)S(1)} %bitcast.179), channel_id=1, source_target_pairs={{0,4},{2,6},{4,0},{6,2},{1,5},{3,7},{5,1},{7,3},{8,12},{10,14},{12... | collective-permute-start | bytes 1889288 | tf_op jit(solution)/shard_map/ppermute | solution.py:55
  17.9 30.1 %collective-permute-start.2 = (bf16[1,120,2624]{2,1,0:T(8,128)(2,1)S(1)}, bf16[1,120,2624]{2,1,0:T(8,128)(2,1)}, u32[]{:S(2)}, u32[]{:S(2)}) collective-permute-start(bf16[1,120,2624]{2,1,0:T(8,128)(2,1)S(1)} %bitcast.180), channel_id=1, source_target_pairs={{0,2},{2,4},{4,6},{6,0},{1,3},{3,5},{5,7},{7,1},{8,10},{10,12},{12... | collective-permute-start | bytes 1889288 | tf_op jit(solution)/shard_map/ppermute | solution.py:55
  20.3 39.6 %collective-permute-start.4 = (bf16[128,960]{1,0:T(8,128)(2,1)S(1)}, bf16[128,960]{1,0:T(8,128)(2,1)S(1)}, u32[]{:S(2)}, u32[]{:S(2)}) collective-permute-start(bf16[128,960]{1,0:T(8,128)(2,1)S(1)} %bitcast.188), channel_id=1, source_target_pairs={{0,6},{2,0},{4,2},{6,4},{1,7},{3,1},{5,3},{7,5},{8,14},{10,8},{12,... | collective-permute-start | bytes 737288 | tf_op jit(solution)/shard_map/ppermute | solution.py:55
  20.3 39.6 %collective-permute-start.5 = (bf16[128,960]{1,0:T(8,128)(2,1)S(1)}, bf16[128,960]{1,0:T(8,128)(2,1)S(1)}, u32[]{:S(2)}, u32[]{:S(2)}) collective-permute-start(bf16[128,960]{1,0:T(8,128)(2,1)S(1)} %bitcast.189), channel_id=1, source_target_pairs={{0,4},{2,6},{4,0},{6,2},{1,5},{3,7},{5,1},{7,3},{8,12},{10,14},{12... | collective-permute-start | bytes 737288 | tf_op jit(solution)/shard_map/ppermute | solution.py:55
  27.3 74.2 %all-to-all-start = ((bf16[8,120,640]{2,1,0:T(8,128)(2,1)}), bf16[8,120,640]{2,1,0:T(8,128)(2,1)S(1)}, u32[]{:S(2)}, u32[]{:S(2)}) async-start(bf16[8,120,640]{2,1,0:T(8,128)(2,1)} %copy.135), calls=%async_computation | async-start | bytes 2457600 | tf_op jit(solution)/shard_map/all_to_all | solution.py:452
  33.4 37.9 %collective-permute-start.6 = (bf16[128,960]{1,0:T(8,128)(2,1)S(1)}, bf16[128,960]{1,0:T(8,128)(2,1)}, u32[]{:S(2)}, u32[]{:S(2)}) collective-permute-start(bf16[128,960]{1,0:T(8,128)(2,1)S(1)} %bitcast.190), channel_id=1, source_target_pairs={{0,2},{2,4},{4,6},{6,0},{1,3},{3,5},{5,7},{7,1},{8,10},{10,12},{12... | collective-permute-start | bytes 737288 | tf_op jit(solution)/shard_map/ppermute | solution.py:55
  51.4 40.0 %collective-permute-start.3 = (bf16[4,120,2624]{2,1,0:T(8,128)(2,1)}, bf16[4,120,2624]{2,1,0:T(8,128)(2,1)}, u32[]{:S(2)}, u32[]{:S(2)}) collective-permute-start(bf16[4,120,2624]{2,1,0:T(8,128)(2,1)} %pad_maximum_fusion), channel_id=1, source_target_pairs={{0,1},{1,0},{2,3},{3,2},{4,5},{5,4},{6,7},{7,6},{8,9},{9,8},{10,11... | collective-permute-start | bytes 7557128 | tf_op jit(solution)/shard_map/ppermute | solution.py:55
  150.2 14.5 %collective-permute-start.9 = (bf16[128,960]{1,0:T(8,128)(2,1)}, bf16[128,960]{1,0:T(8,128)(2,1)S(1)}, u32[]{:S(2)}, u32[]{:S(2)}) collective-permute-start(bf16[128,960]{1,0:T(8,128)(2,1)} %get-tuple-element.39.h0), channel_id=1, source_target_pairs={{0,4},{2,6},{4,0},{6,2},{1,5},{3,7},{5,1},{7,3},{8,12},{10,14},{12... | collective-permute-start | bytes 737288 | tf_op jit(solution)/shard_map/ppermute | solution.py:55
  189.1 19.5 %collective-permute-start.16 = (bf16[512,960]{0,1:T(8,128)(2,1)}, bf16[512,960]{0,1:T(8,128)(2,1)}, u32[]{:S(2)}, u32[]{:S(2)}) collective-permute-start(bf16[512,960]{0,1:T(8,128)(2,1)} %copy.145), channel_id=1, source_target_pairs={{0,1},{1,0},{2,3},{3,2},{4,5},{5,4},{6,7},{7,6},{8,9},{9,8},{10,11... | collective-permute-start | bytes 2949128 | tf_op jit(solution)/shard_map/ppermute | solution.py:55
  198.1 20.4 %collective-permute-start.12 = (bf16[512,960]{0,1:T(8,128)(2,1)}, bf16[512,960]{0,1:T(8,128)(2,1)}, u32[]{:S(2)}, u32[]{:S(2)}) collective-permute-start(bf16[512,960]{0,1:T(8,128)(2,1)} %copy.143), channel_id=1, source_target_pairs={{0,1},{1,0},{2,3},{3,2},{4,5},{5,4},{6,7},{7,6},{8,9},{9,8},{10,11... | collective-permute-start | bytes 2949128 | tf_op jit(solution)/shard_map/ppermute | solution.py:55
  199.7 27.5 %all-to-all-start.1 = ((bf16[8,120,640]{2,1,0:T(8,128)(2,1)}), bf16[8,120,640]{2,1,0:T(8,128)(2,1)S(1)}, u32[]{:S(2)}, u32[]{:S(2)}) async-start(bf16[8,120,640]{2,1,0:T(8,128)(2,1)} %pad_maximum_fusion.1), calls=%async_computation.1 | async-start | bytes 2457600 | tf_op jit(solution)/shard_map/all_to_all | solution.py:480
  205.2 158.2 %all-reduce.3.cloned.1.call-start = ((), (), s32[]{:S(2)}) async-start(), calls=%async_computation.3 | async-start | bytes 3768320 | tf_op jit(solution)/shard_map/psum | solution.py:482
  213.8 14.5 %collective-permute-start.17 = (bf16[128,960]{1,0:T(8,128)(2,1)}, bf16[128,960]{1,0:T(8,128)(2,1)S(1)}, u32[]{:S(2)}, u32[]{:S(2)}) collective-permute-start(bf16[128,960]{1,0:T(8,128)(2,1)} %get-tuple-element.143), channel_id=1, source_target_pairs={{0,2},{2,4},{4,6},{6,0},{1,3},{3,5},{5,7},{7,1},{8,10},{10,12},{12... | collective-permute-start | bytes 737288 | tf_op jit(solution)/shard_map/ppermute | solution.py:55
  216.0 17.6 %collective-permute-start.19 = (bf16[128,960]{1,0:T(8,128)(2,1)}, bf16[128,960]{1,0:T(8,128)(2,1)}, u32[]{:S(2)}, u32[]{:S(2)}) collective-permute-start(bf16[128,960]{1,0:T(8,128)(2,1)} %get-tuple-element.141), channel_id=1, source_target_pairs={{0,6},{2,0},{4,2},{6,4},{1,7},{3,1},{5,3},{7,5},{8,14},{10,8},{12,... | collective-permute-start | bytes 737288 | tf_op jit(solution)/shard_map/ppermute | solution.py:55
  223.7 52.0 %collective-permute-start.13 = (bf16[128,960]{1,0:T(8,128)(2,1)}, bf16[128,960]{1,0:T(8,128)(2,1)S(1)}, u32[]{:S(2)}, u32[]{:S(2)}) collective-permute-start(bf16[128,960]{1,0:T(8,128)(2,1)} %get-tuple-element.145), channel_id=1, source_target_pairs={{0,2},{2,4},{4,6},{6,0},{1,3},{3,5},{5,7},{7,1},{8,10},{10,12},{12... | collective-permute-start | bytes 737288 | tf_op jit(solution)/shard_map/ppermute | solution.py:55
  223.7 53.5 %collective-permute-start.14 = (bf16[128,960]{1,0:T(8,128)(2,1)}, bf16[128,960]{1,0:T(8,128)(2,1)}, u32[]{:S(2)}, u32[]{:S(2)}) collective-permute-start(bf16[128,960]{1,0:T(8,128)(2,1)} %get-tuple-element.147), channel_id=1, source_target_pairs={{0,4},{2,6},{4,0},{6,2},{1,5},{3,7},{5,1},{7,3},{8,12},{10,14},{12... | collective-permute-start | bytes 737288 | tf_op jit(solution)/shard_map/ppermute | solution.py:55
  228.3 51.7 %collective-permute-start.15 = (bf16[128,960]{1,0:T(8,128)(2,1)}, bf16[128,960]{1,0:T(8,128)(2,1)S(1)}, u32[]{:S(2)}, u32[]{:S(2)}) collective-permute-start(bf16[128,960]{1,0:T(8,128)(2,1)} %get-tuple-element.146), channel_id=1, source_target_pairs={{0,6},{2,0},{4,2},{6,4},{1,7},{3,1},{5,3},{7,5},{8,14},{10,8},{12,... | collective-permute-start | bytes 737288 | tf_op jit(solution)/shard_map/ppermute | solution.py:55
  269.6 75.9 %collective-permute-start.32 = (bf16[4,120,1600]{2,1,0:T(8,128)(2,1)}, bf16[4,120,1600]{2,1,0:T(8,128)(2,1)}, u32[]{:S(2)}, u32[]{:S(2)}) collective-permute-start(bf16[4,120,1600]{2,1,0:T(8,128)(2,1)} %fusion.3), channel_id=1, source_target_pairs={{0,1},{1,0},{2,3},{3,2},{4,5},{5,4},{6,7},{7,6},{8,9},{9,8},{10,11... | collective-permute-start | bytes 4608008 | tf_op jit(solution)/shard_map/ppermute | solution.py:55
  272.7 65.7 %collective-permute-start.36 = (bf16[4,120,960]{2,1,0:T(8,128)(2,1)}, bf16[4,120,960]{2,1,0:T(8,128)(2,1)}, u32[]{:S(2)}, u32[]{:S(2)}) collective-permute-start(bf16[4,120,960]{2,1,0:T(8,128)(2,1)} %dynamic-slice_bitcast_fusion), channel_id=1, source_target_pairs={{0,1},{1,0},{2,3},{3,2},{4,5},{5,4},{6,7},{7,6},{8,9},{9,8},{10,11... | collective-permute-start | bytes 2764808 | tf_op jit(solution)/shard_map/ppermute | solution.py:55
  277.3 19.7 %collective-permute-start.21 = (bf16[256,640]{1,0:T(8,128)(2,1)}, bf16[256,640]{1,0:T(8,128)(2,1)}, u32[]{:S(2)}, u32[]{:S(2)}) collective-permute-start(bf16[256,640]{1,0:T(8,128)(2,1)} %get-tuple-element.132), channel_id=1, source_target_pairs={{0,64},{32,96},{64,0},{96,32},{1,65},{33,97},{65,1},{97,33},{2,66}... | collective-permute-start | bytes 983048 | tf_op jit(solution)/shard_map/ppermute | solution.py:55
  280.0 20.0 %collective-permute-start.22 = (bf16[256,640]{1,0:T(8,128)(2,1)}, bf16[256,640]{1,0:T(8,128)(2,1)}, u32[]{:S(2)}, u32[]{:S(2)}) collective-permute-start(bf16[256,640]{1,0:T(8,128)(2,1)} %get-tuple-element.131), channel_id=1, source_target_pairs={{0,96},{32,0},{64,32},{96,64},{1,97},{33,1},{65,33},{97,65},{2,98}... | collective-permute-start | bytes 983048 | tf_op jit(solution)/shard_map/ppermute | solution.py:55
  287.4 15.2 %collective-permute-start.26 = (bf16[256,640]{1,0:T(8,128)(2,1)S(1)}, bf16[256,640]{1,0:T(8,128)(2,1)S(1)}, u32[]{:S(2)}, u32[]{:S(2)}) collective-permute-start(bf16[256,640]{1,0:T(8,128)(2,1)S(1)} %get-tuple-element.133), channel_id=1, source_target_pairs={{0,8},{8,16},{16,24},{24,0},{1,9},{9,17},{17,25},{25,1},{2,10},{10... | collective-permute-start | bytes 983048 | tf_op jit(solution)/shard_map/ppermute | solution.py:55
  300.0 20.4 %collective-permute-start.28 = (bf16[256,640]{1,0:T(8,128)(2,1)S(1)}, bf16[256,640]{1,0:T(8,128)(2,1)S(1)}, u32[]{:S(2)}, u32[]{:S(2)}) collective-permute-start(bf16[256,640]{1,0:T(8,128)(2,1)S(1)} %get-tuple-element.134), channel_id=1, source_target_pairs={{0,24},{8,0},{16,8},{24,16},{1,25},{9,1},{17,9},{25,17},{2,26},{10... | collective-permute-start | bytes 983048 | tf_op jit(solution)/shard_map/ppermute | solution.py:55
  302.6 21.5 %collective-permute-start.23 = (bf16[64,640]{1,0:T(8,128)(2,1)S(1)}, bf16[64,640]{1,0:T(8,128)(2,1)S(1)}, u32[]{:S(2)}, u32[]{:S(2)}) collective-permute-start(bf16[64,640]{1,0:T(8,128)(2,1)S(1)} %get-tuple-element.154), channel_id=1, source_target_pairs={{0,8},{8,16},{16,24},{24,0},{1,9},{9,17},{17,25},{25,1},{2,10},{10... | collective-permute-start | bytes 245768 | tf_op jit(solution)/shard_map/ppermute | solution.py:55
  308.0 16.1 %collective-permute-start.24 = (bf16[64,640]{1,0:T(8,128)(2,1)S(1)}, bf16[64,640]{1,0:T(8,128)(2,1)S(1)}, u32[]{:S(2)}, u32[]{:S(2)}) collective-permute-start(bf16[64,640]{1,0:T(8,128)(2,1)S(1)} %get-tuple-element.156), channel_id=1, source_target_pairs={{0,16},{8,24},{16,0},{24,8},{1,17},{9,25},{17,1},{25,9},{2,18},{10... | collective-permute-start | bytes 245768 | tf_op jit(solution)/shard_map/ppermute | solution.py:55
  340.5 17.6 %collective-permute-start.38 = (bf16[120,960]{1,0:T(8,128)(2,1)S(1)}, bf16[120,960]{1,0:T(8,128)(2,1)S(1)}, u32[]{:S(2)}, u32[]{:S(2)}) collective-permute-start(bf16[120,960]{1,0:T(8,128)(2,1)S(1)} %get-tuple-element.150), channel_id=1, source_target_pairs={{0,4},{2,6},{4,0},{6,2},{1,5},{3,7},{5,1},{7,3},{8,12},{10,14},{12... | collective-permute-start | bytes 691208 | tf_op jit(solution)/shard_map/ppermute | solution.py:55
  345.5 17.8 %collective-permute-start.39 = (bf16[120,960]{1,0:T(8,128)(2,1)S(1)}, bf16[120,960]{1,0:T(8,128)(2,1)S(1)}, u32[]{:S(2)}, u32[]{:S(2)}) collective-permute-start(bf16[120,960]{1,0:T(8,128)(2,1)S(1)} %get-tuple-element.149), channel_id=1, source_target_pairs={{0,6},{2,0},{4,2},{6,4},{1,7},{3,1},{5,3},{7,5},{8,14},{10,8},{12,... | collective-permute-start | bytes 691208 | tf_op jit(solution)/shard_map/ppermute | solution.py:55
  349.6 26.2 %collective-permute-start.33 = (bf16[120,1600]{1,0:T(8,128)(2,1)}, bf16[120,1600]{1,0:T(8,128)(2,1)}, u32[]{:S(2)}, u32[]{:S(2)}) collective-permute-start(bf16[120,1600]{1,0:T(8,128)(2,1)} %get-tuple-element.127), channel_id=1, source_target_pairs={{0,2},{2,4},{4,6},{6,0},{1,3},{3,5},{5,7},{7,1},{8,10},{10,12},{12... | collective-permute-start | bytes 1152008 | tf_op jit(solution)/shard_map/ppermute | solution.py:55
  351.7 24.2 %collective-permute-start.34 = (bf16[120,1600]{1,0:T(8,128)(2,1)}, bf16[120,1600]{1,0:T(8,128)(2,1)}, u32[]{:S(2)}, u32[]{:S(2)}) collective-permute-start(bf16[120,1600]{1,0:T(8,128)(2,1)} %get-tuple-element.129), channel_id=1, source_target_pairs={{0,4},{2,6},{4,0},{6,2},{1,5},{3,7},{5,1},{7,3},{8,12},{10,14},{12... | collective-permute-start | bytes 1152008 | tf_op jit(solution)/shard_map/ppermute | solution.py:55
  352.9 23.0 %collective-permute-start.35 = (bf16[120,1600]{1,0:T(8,128)(2,1)}, bf16[120,1600]{1,0:T(8,128)(2,1)}, u32[]{:S(2)}, u32[]{:S(2)}) collective-permute-start(bf16[120,1600]{1,0:T(8,128)(2,1)} %get-tuple-element.128), channel_id=1, source_target_pairs={{0,6},{2,0},{4,2},{6,4},{1,7},{3,1},{5,3},{7,5},{8,14},{10,8},{12,... | collective-permute-start | bytes 1152008 | tf_op jit(solution)/shard_map/ppermute | solution.py:55
  (57 other events, 501.4 us)
Sparse Core Ops, SparseCore 0:
  10.2 53.4 all-gather.2
  228.4 97.4 all-reduce.2
